TPU v7x, 256 devices: a whole 4x4x8 slice. The times are simulated.
256 devices in a mesh: pool: 32 (over y, x, core), head: 8 (over z).
Axes of the slice: x: 4, y: 4, z: 8, core: 2. Of those that a mesh axis runs over, the one named last changes fastest.
Arguments:
- queries: bfloat16 [32, 8, 2048], P('pool', 'head')
- keys: bfloat16 [2048, 8, 256, 128], P('pool', 'head'), may hold values from -6 to 6
- values: bfloat16 [2048, 8, 256, 128], P('pool', 'head'), may hold values from -6 to 6
- page_table: int32 [32, 64], replicated, may hold values from -1 to 2047, as said below
- lengths: int32 [32], replicated, may hold values from 1 to 16384, as said below
Outputs:
- attended: bfloat16 [32, 8, 2048], P('pool', 'head')
Inputs may be any that keep to these rules, and one draw needn't show every extreme that they name: `page_table`: each request names its pages in entries 0 .. ceil(lengths / 256) - 1 and -1 after them; no pool page is named twice; some request has exactly 64 pages. `lengths`: some request has exactly 16384 tokens.
All inputs are finite; a program needn't handle non-finite values.
Results may differ from a plain program's by a relative error of at most 0.015.
Values may be sent and summed in bfloat16 or wider, within the bound.
No kernel may reach another device: no remote copies, remote signals or barrier semaphores. Data moves between devices by JAX's collectives and lax.ppermute only.
A program may use at most 64 MiB of HBM per device.

v0:
```python
import jax
import jax.numpy as jnp
from jax import lax
from jax.sharding import PartitionSpec as P


def combined_all(array, axis, combine):
    everything = jax.tree.map(lambda part: lax.all_gather(part, axis), array)
    leading = jax.tree.map(lambda part: part[0], everything)

    def lap(k, so_far):
        return combine(so_far, jax.tree.map(lambda part: part[k], everything))

    return lax.fori_loop(1, lax.axis_size(axis), lap, leading)


def join(first, second):
    max_a, sum_a, acc_a = first
    max_b, sum_b, acc_b = second
    joined = jnp.maximum(max_a, max_b)
    fac_a = jnp.exp(max_a - joined)
    fac_b = jnp.exp(max_b - joined)
    return (
        joined,
        sum_a * fac_a + sum_b * fac_b,
        acc_a * fac_a[..., None] + acc_b * fac_b[..., None],
    )


def per_device(queries, keys, values, page_table, lengths):
    local_pages, kv_local, page_len, head_dim = keys.shape
    rows = queries.shape[0]
    group = queries.shape[2] // head_dim
    requests = page_table.shape[0]
    most_pages = page_table.shape[1]
    scale = head_dim ** (-0.5)
    gathered = lax.all_gather(queries, "pool", axis=0, tiled=True)
    query_all = gathered.reshape(requests, kv_local, group, head_dim)
    first_slot = lax.axis_index("pool") * local_pages
    slot_ids = first_slot + jnp.arange(local_pages, dtype=jnp.int32)
    match = page_table[:, :, None] == slot_ids[None, None, :]
    request_ids = jnp.arange(requests, dtype=jnp.int32)
    owner = jnp.sum(jnp.where(match, request_ids[:, None, None], 0), axis=(0, 1))
    page_pos = jnp.sum(
        jnp.where(match, jnp.arange(most_pages, dtype=jnp.int32)[None, :, None], 0), axis=(0, 1)
    )
    valid = jnp.any(match, axis=(0, 1))
    onehot = (request_ids[:, None] == owner[None, :]) & valid[None, :]
    selected = query_all[owner]
    scores = (
        jnp.einsum("pkgd,pktd->pkgt", selected, keys, preferred_element_type=jnp.float32) * scale
    )
    positions = page_pos[:, None] * page_len + jnp.arange(page_len, dtype=jnp.int32)[None, :]
    live = valid[:, None] & (positions < lengths[owner][:, None])
    live_wide = live[:, None, None, :]
    scores = jnp.where(live_wide, scores, -1e30)
    page_max = jnp.max(scores, axis=-1)
    local_max = jnp.max(jnp.where(onehot[:, :, None, None], page_max[None], -1e30), axis=1)
    shifted = local_max[owner]
    weights = jnp.where(live_wide, jnp.exp(scores - shifted[..., None]), 0.0)
    page_sum = jnp.sum(weights, axis=-1)
    rounded = weights.astype(jnp.bfloat16)
    partial_value = jnp.einsum(
        "pkgt,pktd->pkgd", rounded, values, preferred_element_type=jnp.float32
    )
    selector = onehot.astype(jnp.float32)
    local_sum = jnp.dot(
        selector, page_sum.reshape(local_pages, -1), precision=lax.Precision.HIGHEST
    ).reshape(requests, kv_local, group)
    local_acc = jnp.dot(
        selector, partial_value.reshape(local_pages, -1), precision=lax.Precision.HIGHEST
    ).reshape(requests, kv_local, group, head_dim)
    start = lax.axis_index("pool") * rows
    merged = combined_all((local_max, local_sum, local_acc), "pool", join)
    total = lax.dynamic_slice_in_dim(merged[1], start, rows, 0)
    numer = lax.dynamic_slice_in_dim(merged[2], start, rows, 0)
    result = numer / total[..., None]
    return result.reshape(rows, kv_local, group * head_dim).astype(jnp.bfloat16)


def solution(mesh):
    placed = (
        P("pool", "head", None),
        P("pool", "head", None, None),
        P("pool", "head", None, None),
        P(),
        P(),
    )
    return jax.shard_map(
        per_device, mesh=mesh, in_specs=placed, out_specs=P("pool", "head", None), check_vma=False
    )
```

profile of v0, /device:TPU:1, one launch (start us, length us, event | category | flops | bytes accessed | tf_op | source)
XLA Modules:
  0.0 160.7 jit_solution(4433840381757552678)
XLA Ops:
  6.5 1.1 compare_reduce_fusion
  7.6 1.1 fusion.17
  8.7 26.4 %all_gather.15 = bf16[32,1,2048]{2,1,0:T(2,128)(2,1)S(1)} all-gather(bf16[1,1,2048]{2,1,0:T(2,128)(2,1)} %param.7), channel_id=1, replica_groups=mesh['pool'=32,'head'=8] {'pool'}, dimensions={0}, use_global_device_ids=true | all-gather | bytes 135168 | tf_op jit(solution)/shard_map/all_gather | solution.py:37
  37.5 3.5 %fusion.37 = (f32[64,16]{1,0:T(8,128)S(1)}, f32[64,16,256]{2,1,0:T(8,128)S(1)}) fusion(bf16[64,16,128]{2,1,0:T(8,128)(2,1)S(1)} %gather_fusion.1, bf16[64,1,256,128]{3,2,1,0:T(8,128)(2,1)} %param.8, pred[64,256]{1,0:T(8,128)(4,1)S(1)} %fusion.27), kind=kOutput, calls=%fused_computation.58 | convolution fusion | flops 67894272 | bytes 5525504 | tf_op jit(solution)/shard_map/pkgd,pktd->pkgt/dot_general | solution.py:51
  41.8 3.0 %fusion.6 = f32[64,16,128]{2,1,0:T(8,128)S(1)} fusion(bf16[64,1,256,128]{3,2,1,0:T(8,128)(2,1)} %param.9, f32[64,16,256]{2,1,0:T(8,128)S(1)} %get-tuple-element.240, f32[64,16]{1,0:T(8,128)S(1)} %gather_fusion.2, pred[64,256]{1,0:T(8,128)(4,1)S(1)} %fusion.27), kind=kOutput, calls=%fused_computation.15 | convolution fusion | flops 67895296 | bytes 5787648 | tf_op jit(solution)/shard_map/pkgt,pktd->pkgd/dot_general | solution.py:63
  44.8 1.2 fusion.21
  46.6 24.1 %all-gather.4 = f32[32,32,16]{1,2,0:T(8,128)S(1)} all-gather(f32[1,32,16]{1,2,0:T(8,128)S(1)} %convolution_bitcast_fusion), channel_id=3, replica_groups=mesh['pool'=32,'head'=8] {'pool'}, dimensions={0}, use_global_device_ids=true | all-gather | bytes 67584 | tf_op jit(solution)/shard_map/all_gather | solution.py:8
  70.8 22.5 %all-gather.3 = f32[32,32,16]{1,2,0:T(8,128)S(1)} all-gather(f32[1,32,16]{1,2,0:T(8,128)S(1)} %copy.40), channel_id=2, replica_groups=mesh['pool'=32,'head'=8] {'pool'}, dimensions={0}, use_global_device_ids=true | all-gather | bytes 67584 | tf_op jit(solution)/shard_map/all_gather | solution.py:8
  93.3 12.0 %all-gather.7.cloned.1.call-done = f32[1024,16,128]{2,0,1:T(8,128)} async-done(((f32[32,16,128]{2,0,1:T(8,128)}), f32[1024,16,128]{2,0,1:T(8,128)}) %all-gather.7.cloned.1.call-update) | async-done | bytes 8388624 | tf_op jit(solution)/shard_map/all_gather | solution.py:8
  106.4 46.6 %while.19 = (s32[]{:T(128)}, f32[32,1,16]{0,2,1:T(8,128)S(1)}, f32[32,1,16]{0,2,1:T(8,128)S(1)}, f32[32,1,16,128]{3,2,1,0:T(8,128)S(1)}, f32[32,32,1,16]{1,3,2,0...) while((s32[]{:T(128)}, f32[32,1,16]{0,2,1:T(8,128)S(1)}, ...), condition=%wide.region_7.8_spmd, body=%wide.region_6.7_spmd.sunk | while | flops 200197 | bytes 1349779 | solution.py:14
  106.6 1.0 constant_dynamic-slice_fusion.2
  108.1 1.0 constant_dynamic-slice_fusion.2
  109.6 1.0 constant_dynamic-slice_fusion.2
  111.1 1.0 constant_dynamic-slice_fusion.2
  112.6 1.0 constant_dynamic-slice_fusion.2
  114.1 1.0 constant_dynamic-slice_fusion.2
  115.6 1.0 constant_dynamic-slice_fusion.2
  117.2 1.0 constant_dynamic-slice_fusion.2
  118.7 1.0 constant_dynamic-slice_fusion.2
  120.2 1.0 constant_dynamic-slice_fusion.2
  121.7 1.0 constant_dynamic-slice_fusion.2
  123.2 1.0 constant_dynamic-slice_fusion.2
  124.7 1.0 constant_dynamic-slice_fusion.2
  127.7 1.0 constant_dynamic-slice_fusion.2
  (230 shorter events, 37.3 us)
Async XLA Ops:
  6.5 29.4 %copy-start = (s32[32]{0:T(128)S(1)}, s32[32]{0:T(128)}, u32[]{:S(2)}) copy-start(s32[32]{0:T(128)} %param.11) | copy-start | bytes 388
  6.5 98.7 %all-gather.7.cloned.1.call-start = ((), (), s32[]{:S(2)}) async-start(), calls=%async_computation | async-start | bytes 8650752 | tf_op jit(solution)/shard_map/all_gather | solution.py:8
Sparse Core Ops, SparseCore 0:
  46.1 59.1 all-gather.6
where the time goes:
time: 162 us; the launch traced here: 161 us
  blocking collectives  73.1 us (45%)
  local copies, waits for them, and re-layouts  38.9 us (24%)
  other arithmetic  14 us (9%)
  between operations  13.5 us (8%)
  waiting for transfers between devices  12 us (7%)
  matrix products  7.81 us (5%)
    all_gather x2, blocking collectives, combined_all(): everything = jax.tree.map(lambda part: lax.all_gather(part, axis), array)  46.7 us
    dynamic_slice x31, local copies, waits for them, and re-layouts, lap(): return combine(so_far, jax.tree.map(lambda part: part[k], everything))  30.1 us
    all_gather x1, blocking collectives, per_device(): gathered = lax.all_gather(queries, 'pool', axis=0, tiled=True)  26.4 us
    all_gather x1, waiting for transfers between devices, combined_all(): everything = jax.tree.map(lambda part: lax.all_gather(part, axis), array)  12 us
    add x31, other arithmetic, join(): acc_a * fac_a[..., None] + acc_b * fac_b[..., None]  9.37 us
    dot_general x1, matrix products, per_device(): jnp.einsum('pkgd,pktd->pkgt', selected, keys, preferred_element_type=jnp....  3.47 us
  transfers between devices with their start and end apart: 1, of which 1 were waited for; matrix products, arithmetic and copies ran while one was open for 0% of the time, Pallas kernels for 0%

commit v1 on v0

v1 whole, which is shorter than its diff:
```python
import jax
import jax.numpy as jnp
from jax import lax
from jax.experimental import pallas as pl
from jax.experimental.pallas import tpu as pltpu
from jax.sharding import PartitionSpec as P

MASKED = -3.0e38
EMPTY = -1.5e38
STAT_ROWS = 8


def three_parts(x):
    high = x.astype(jnp.bfloat16).astype(jnp.float32)
    rest = x - high
    middle = rest.astype(jnp.bfloat16).astype(jnp.float32)
    return high, middle, rest - middle


def attend_kernel(owner_ref, live_ref, q_ref, k_ref, v_ref, out_ref, s_ref, mx_ref, sum_ref, acc_ref):
    pages, page_len, head_dim = k_ref.shape
    requests, group, _ = q_ref.shape
    factor = head_dim ** (-0.5) * 1.4426950408889634
    token = lax.broadcasted_iota(jnp.int32, (group, page_len), 1)
    halves = page_len // head_dim
    mx_ref[...] = jnp.full(mx_ref.shape, EMPTY, jnp.float32)
    sum_ref[...] = jnp.zeros(sum_ref.shape, jnp.float32)
    acc_ref[...] = jnp.zeros(acc_ref.shape, jnp.float32)

    def score(p, carry):
        owner = owner_ref[p]
        s = lax.dot_general(
            q_ref[owner], k_ref[p], (((1,), (1,)), ((), ())), preferred_element_type=jnp.float32
        )
        s = jnp.where(token < live_ref[p], s, MASKED)
        s_ref[p] = s
        top = s[:, :head_dim]
        for h in range(1, halves):
            top = jnp.maximum(top, s[:, h * head_dim : (h + 1) * head_dim])
        mx_ref[owner] = jnp.maximum(mx_ref[owner], top)
        return carry

    lax.fori_loop(0, pages, score, 0, unroll=8)
    mx_ref[...] = jnp.broadcast_to(jnp.max(mx_ref[...], axis=-1, keepdims=True), mx_ref.shape)

    def weigh(p, carry):
        owner = owner_ref[p]
        top = mx_ref[owner]
        parts = [
            jnp.exp2((s_ref[p, :, h * head_dim : (h + 1) * head_dim] - top) * factor)
            for h in range(halves)
        ]
        sum_ref[owner] += sum(parts)
        weights = jnp.concatenate(parts, axis=1).astype(jnp.bfloat16)
        acc_ref[owner] += jnp.dot(weights, v_ref[p], preferred_element_type=jnp.float32)
        return carry

    lax.fori_loop(0, pages, weigh, 0, unroll=8)
    out_ref[:, :group, :] = acc_ref[...].astype(jnp.bfloat16)
    total = jnp.broadcast_to(jnp.sum(sum_ref[...], axis=-1, keepdims=True), sum_ref.shape)
    lane = lax.broadcasted_iota(jnp.int32, sum_ref.shape, 2)
    row = lax.broadcasted_iota(jnp.int32, sum_ref.shape, 1)
    stats = jnp.zeros(sum_ref.shape, jnp.float32)
    for k, part in enumerate(three_parts(mx_ref[...]) + three_parts(total)):
        stats = jnp.where(lane == row + k * group, part, stats)
    stats = jnp.sum(stats, axis=1, keepdims=True)
    out_ref[:, group:, :] = jnp.broadcast_to(stats, (requests, STAT_ROWS, head_dim)).astype(jnp.bfloat16)


def join_kernel(parts_ref, out_ref, *, group, factor):
    sources, _, head_dim = parts_ref.shape
    stats = parts_ref[:, group:, :].astype(jnp.float32)[:, 0, :]
    peak = stats[:, :group] + stats[:, group : 2 * group] + stats[:, 2 * group : 3 * group]
    total = (
        stats[:, 3 * group : 4 * group] + stats[:, 4 * group : 5 * group] + stats[:, 5 * group : 6 * group]
    )
    weight = jnp.exp2((peak - jnp.max(peak, axis=0, keepdims=True)) * factor)
    weight = weight / jnp.sum(weight * total, axis=0, keepdims=True)
    weight = weight.T
    result = jnp.zeros((group, head_dim), jnp.float32)
    for s in range(sources):
        result += weight[:, s : s + 1] * parts_ref[s, :group, :].astype(jnp.float32)
    for g in range(group):
        out_ref[0, :, g * head_dim : (g + 1) * head_dim] = result[g : g + 1, :].astype(jnp.bfloat16)


def per_device(queries, keys, values, page_table, lengths):
    pages, _, page_len, head_dim = keys.shape
    group = queries.shape[2] // head_dim
    requests, most_pages = page_table.shape
    factor = head_dim ** (-0.5) * 1.4426950408889634
    spread = jnp.broadcast_to(queries.reshape(1, group, head_dim), (requests, group, head_dim))
    query_all = lax.all_to_all(spread, "pool", 0, 0, tiled=True)
    slot_ids = lax.axis_index("pool") * pages + jnp.arange(pages, dtype=jnp.int32)
    match = page_table[:, :, None] == slot_ids[None, None, :]
    request_ids = jnp.arange(requests, dtype=jnp.int32)
    left = lengths[:, None] - page_len * jnp.arange(most_pages, dtype=jnp.int32)[None, :]
    owner = jnp.sum(jnp.where(match, request_ids[:, None, None], 0), axis=(0, 1))
    live = jnp.sum(jnp.where(match, left[:, :, None], 0), axis=(0, 1))
    vmem = pl.BlockSpec(memory_space=pltpu.VMEM)
    smem = pl.BlockSpec(memory_space=pltpu.SMEM)
    partial = pl.pallas_call(
        attend_kernel,
        out_shape=jax.ShapeDtypeStruct((requests, group + STAT_ROWS, head_dim), jnp.bfloat16),
        in_specs=[smem, smem, vmem, vmem, vmem],
        out_specs=vmem,
        scratch_shapes=[
            pltpu.VMEM((pages, group, page_len), jnp.float32),
            pltpu.VMEM((requests, group, head_dim), jnp.float32),
            pltpu.VMEM((requests, group, head_dim), jnp.float32),
            pltpu.VMEM((requests, group, head_dim), jnp.float32),
        ],
        compiler_params=pltpu.CompilerParams(vmem_limit_bytes=24 * 1024 * 1024),
    )(owner, live, query_all, keys.reshape(pages, page_len, head_dim), values.reshape(pages, page_len, head_dim))
    received = lax.all_to_all(partial, "pool", 0, 0, tiled=True)

    def join(parts_ref, out_ref):
        join_kernel(parts_ref, out_ref, group=group, factor=factor)

    return pl.pallas_call(
        join,
        out_shape=jax.ShapeDtypeStruct((1, 1, group * head_dim), jnp.bfloat16),
        in_specs=[vmem],
        out_specs=vmem,
    )(received)


def solution(mesh):
    placed = (
        P("pool", "head", None),
        P("pool", "head", None, None),
        P("pool", "head", None, None),
        P(),
        P(),
    )
    return jax.shard_map(
        per_device, mesh=mesh, in_specs=placed, out_specs=P("pool", "head", None), check_vma=False
    )
```

time: 162 us -> 41 us (0.25)
  blocking collectives: 73.1 us -> 12 us
  local copies, waits for them, and re-layouts: 38.9 us -> 5.03 us
  between operations: 13.5 us -> 0.05 us
  other arithmetic: 14 us -> 2.86 us
  starting transfers between devices: 0.01 us -> 8.59 us
  matrix products: 7.81 us -> 0 us
  Pallas kernels: 0 us -> 6.59 us
  waiting for transfers between devices: 12 us -> 5.46 us
    all_gather x3 -> x0, blocking collectives: 73.1 us -> none  [the longest x2 46.7 us: combined_all(): everything = jax.tree.map(lambda part: lax.all_gather(part, axis), array)]
    dynamic_slice x32 -> x0, local copies, waits for them, and re-layouts: 30.3 us -> none  [the longest x31 30.1 us: lap(): return combine(so_far, jax.tree.map(lambda part: part[k], everything))]
    all_to_all x0 -> x1, blocking collectives: none -> 12 us  [per_device(): received = lax.all_to_all(partial, 'pool', 0, 0, tiled=True)]
    all_gather x1 -> x0, waiting for transfers between devices: 12 us -> none  [combined_all(): everything = jax.tree.map(lambda part: lax.all_gather(part, axis), array)]
    add x32 -> x1, other arithmetic: 9.37 us -> 0.01 us  [per_device(): lax.axis_index('pool') * pages + jnp.arange(pages, dtype=jnp.int32)]
    all_to_all x0 -> x1, starting transfers between devices: none -> 8.59 us  [per_device(): query_all = lax.all_to_all(spread, 'pool', 0, 0, tiled=True)]
    dot_general x4 -> x0, matrix products: 7.81 us -> none  [the longest x1 3.47 us: per_device(): jnp.einsum('pkgd,pktd->pkgt', selected, keys, preferred_element_type=jnp....]
    pallas_call x0 -> x2, Pallas kernels: none -> 6.59 us  [the longest x1 4.6 us: per_device(): pl.pallas_call(attend_kernel, out_shape=jax.ShapeDtypeStruct((requests, g...]
  transfers between devices with their start and end apart: 1 -> 1, of which waited for: 1 -> 1; matrix products, arithmetic and copies ran while one was open for 0% -> 5% of each run, Pallas kernels for 0% -> 0%
where the time goes in v1:
time: 41 us; the launch traced here: 40.6 us
  blocking collectives  12 us (29%)
  starting transfers between devices  8.59 us (21%)
  Pallas kernels  6.59 us (16%)
  waiting for transfers between devices  5.46 us (13%)
  local copies, waits for them, and re-layouts  5.03 us (12%)
  other arithmetic  2.86 us (7%)
    all_to_all x1, blocking collectives, per_device(): received = lax.all_to_all(partial, 'pool', 0, 0, tiled=True)  12 us
    all_to_all x1, starting transfers between devices, per_device(): query_all = lax.all_to_all(spread, 'pool', 0, 0, tiled=True)  8.59 us
    all_to_all x1, waiting for transfers between devices, per_device(): query_all = lax.all_to_all(spread, 'pool', 0, 0, tiled=True)  5.46 us
    pallas_call x1, Pallas kernels, per_device(): pl.pallas_call(attend_kernel, out_shape=jax.ShapeDtypeStruct((requests, g...  4.6 us
    unnamed x4, local copies, waits for them, and re-layouts  4.38 us
    pallas_call x1, Pallas kernels, per_device(): pl.pallas_call(join, out_shape=jax.ShapeDtypeStruct((1, 1, group * head_d...  1.99 us
    reduce_sum x1, other arithmetic, per_device(): live = jnp.sum(jnp.where(match, left[:, :, None], 0), axis=(0, 1))  1.4 us
  transfers between devices with their start and end apart: 1, of which 1 were waited for; matrix products, arithmetic and copies ran while one was open for 5% of the time, Pallas kernels for 0%

profile of v1, /device:TPU:1, one launch (start us, length us, event | category | flops | bytes accessed | tf_op | source)
XLA Modules:
  0.0 40.6 jit_solution(13776801124193192423)
XLA Ops:
  0.0 0.7 %reduce = bf16[2048]{0:T(1024)(128)(2,1)S(1)} reduce(bf16[1,1,2048]{2,1,0:T(2,128)(2,1)} %param.5, bf16[]{:T(256)} %constant.15), dimensions={0,1}, to_apply=%param.5.reduce_sub_computation | reduce | bytes 8194 | tf_op args[0]
  0.7 0.7 %broadcast_in_dim.39 = bf16[32,16,128]{2,1,0:T(8,128)(2,1)} broadcast(bf16[16,128]{1,0:T(8,128)(2,1)S(1)} %bitcast.5), dimensions={1,2} | broadcast | bytes 135168 | tf_op jit(solution)/shard_map/broadcast_in_dim | solution.py:92
  1.4 8.6 %all-to-all-start = ((bf16[32,16,128]{2,1,0:T(8,128)(2,1)}), bf16[32,16,128]{2,1,0:T(8,128)(2,1)S(1)}, u32[]{:S(2)}, u32[]{:S(2)}) async-start(bf16[32,16,128]{2,1,0:T(8,128)(2,1)} %broadcast_in_dim.39), calls=%async_computation | async-start | bytes 262144 | tf_op jit(solution)/shard_map/all_to_all | solution.py:93
  10.0 0.7 %broadcast_subtract_fusion = s32[32,64]{1,0:T(8,128)S(1)} fusion(s32[64]{0:T(128)S(1)} %iota_multiply_fusion, s32[32]{0:T(128)} %param.9), kind=kLoop, calls=%fused_computation.4 | loop fusion | flops 2048 | bytes 8576 | tf_op jit(solution)/shard_map/sub | solution.py:97
  10.7 1.4 %fusion.1 = (s32[64]{0:T(128)S(1)}, s32[64]{0:T(128)S(1)}) fusion(s32[32,64]{1,0:T(8,128)S(1)} %broadcast_subtract_fusion, s32[64]{0:T(128)S(1)} %iota_add_fusion, s32[32,64]{1,0:T(8,128)} %param.8), kind=kLoop, calls=%fused_computation.3 | loop fusion | flops 655232 | bytes 17152 | tf_op jit(solution)/shard_map/reduce_sum | solution.py:99
  12.1 5.5 %all-to-all-done.q_ref = bf16[32,16,128]{2,1,0:T(8,128)(2,1)S(1)} async-done(((bf16[32,16,128]{2,1,0:T(8,128)(2,1)}), bf16[32,16,128]{2,1,0:T(8,128)(2,1)S(1)}, u32[]{:S(2)}, u32[]{:S(2)}) %all-to-all-start) | async-done | bytes 131104 | tf_op jit(solution)/shard_map/all_to_all | solution.py:93
  17.6 0.0 copy-start
  17.6 2.2 %copy-done = bf16[64,1,256,128]{3,2,1,0:T(8,128)(2,1)S(1)} copy-done((bf16[64,1,256,128]{3,2,1,0:T(8,128)(2,1)S(1)}, bf16[64,1,256,128]{3,2,1,0:T(8,128)(2,1)}, u32[]{:S(2)}) %copy-start) | copy-done | bytes 4194328
  19.8 0.0 copy-start.1
  19.8 2.2 %copy-done.1 = bf16[64,1,256,128]{3,2,1,0:T(8,128)(2,1)S(1)} copy-done((bf16[64,1,256,128]{3,2,1,0:T(8,128)(2,1)S(1)}, bf16[64,1,256,128]{3,2,1,0:T(8,128)(2,1)}, u32[]{:S(2)}) %copy-start.1) | copy-done | bytes 4194328
  22.0 4.6 %shard_map.55 = bf16[32,24,128]{2,1,0:T(8,128)(2,1)S(1)} custom-call(s32[64]{0:T(128)S(1)} %get-tuple-element.6.owner_ref, s32[64]{0:T(128)S(1)} %get-tuple-element.5.live_ref, bf16[32,16,128]{2,1,0:T(8,128)(2,1)S(1)} %all-to-all-done.q_ref, bf16[64,256,128]{2,1,0:T(8,128)(2,1)S(1)} %bitcast.3, bf16[64,256,128]{2,1,0:T(8,128)(2,1)S(1)} %bitcast.4), custom_call_target="tpu_custom_call" | custom-call | tf_op jit(solution)/shard_map/pallas_call | solution.py:102
  26.6 12.0 %all_to_all.10.parts_ref = bf16[32,24,128]{2,1,0:T(8,128)(2,1)} all-to-all(bf16[32,24,128]{2,1,0:T(8,128)(2,1)S(1)} %shard_map.55), channel_id=1, replica_groups=mesh['pool'=32,'head'=8] {'pool'}, dimensions={0} | all-to-all | bytes 393216 | tf_op jit(solution)/shard_map/all_to_all | solution.py:115
  38.6 2.0 %shard_map.56 = bf16[1,1,2048]{2,1,0:T(2,128)(2,1)} custom-call(bf16[32,24,128]{2,1,0:T(8,128)(2,1)} %all_to_all.10.parts_ref), custom_call_target="tpu_custom_call" | custom-call | tf_op jit(solution)/shard_map/pallas_call | solution.py:120
  (2 shorter events, 0.0 us)
Async XLA Ops:
  1.4 16.2 %all-to-all-start = ((bf16[32,16,128]{2,1,0:T(8,128)(2,1)}), bf16[32,16,128]{2,1,0:T(8,128)(2,1)S(1)}, u32[]{:S(2)}, u32[]{:S(2)}) async-start(bf16[32,16,128]{2,1,0:T(8,128)(2,1)} %broadcast_in_dim.39), calls=%async_computation | async-start | bytes 262144 | tf_op jit(solution)/shard_map/all_to_all | solution.py:93
  17.6 2.2 %copy-start = (bf16[64,1,256,128]{3,2,1,0:T(8,128)(2,1)S(1)}, bf16[64,1,256,128]{3,2,1,0:T(8,128)(2,1)}, u32[]{:S(2)}) copy-start(bf16[64,1,256,128]{3,2,1,0:T(8,128)(2,1)} %param.6) | copy-start | bytes 12582916
  19.8 2.2 %copy-start.1 = (bf16[64,1,256,128]{3,2,1,0:T(8,128)(2,1)S(1)}, bf16[64,1,256,128]{3,2,1,0:T(8,128)(2,1)}, u32[]{:S(2)}) copy-start(bf16[64,1,256,128]{3,2,1,0:T(8,128)(2,1)} %param.7) | copy-start | bytes 12582916

commit v2 on v1

v2 whole, which is shorter than its diff:
```python
import jax
import jax.numpy as jnp
from jax import lax
from jax.experimental import pallas as pl
from jax.experimental.pallas import tpu as pltpu
from jax.sharding import PartitionSpec as P

MASKED = -3.0e38
EMPTY = -1.5e38
STAT_ROWS = 8
CODE = 512
EARLY = 48
CHUNKS = 2
MIB = 1024 * 1024
LOG2E = 1.4426950408889634


def three_parts(x):
    high = x.astype(jnp.bfloat16).astype(jnp.float32)
    rest = x - high
    middle = rest.astype(jnp.bfloat16).astype(jnp.float32)
    return high, middle, rest - middle


def spread_kernel(q_hbm, out_ref, q_ref, sem):
    _, group, head_dim = out_ref.shape
    copy = pltpu.make_async_copy(q_hbm, q_ref, sem)
    copy.start()
    copy.wait()
    rows = [q_ref[0, :, g * head_dim : (g + 1) * head_dim].astype(jnp.float32) for g in range(group)]
    tile = jnp.concatenate(rows, axis=0).astype(jnp.bfloat16)
    out_ref[...] = jnp.broadcast_to(tile[None], out_ref.shape)


def prepare_kernel(length_hbm, table_hbm, k_hbm, code_ref, early_ref, length_ref, table_ref, sems):
    pages, page_len, _ = k_hbm.shape
    requests, most_pages = table_ref.shape
    lengths = pltpu.make_async_copy(length_hbm, length_ref, sems.at[0])
    table = pltpu.make_async_copy(table_hbm, table_ref, sems.at[1])
    early = pltpu.make_async_copy(k_hbm.at[pl.ds(0, early_ref.shape[0])], early_ref, sems.at[2])
    lengths.start()
    table.start()
    early.start()
    lengths.wait()
    table.wait()
    slot = lax.axis_index("pool") * pages + lax.broadcasted_iota(jnp.int32, (pages, most_pages), 0)
    begin = page_len * lax.broadcasted_iota(jnp.int32, (1, most_pages), 1)
    code = jnp.zeros((pages, most_pages), jnp.int32)
    for r in range(requests):
        live = jnp.clip(length_ref[r] - begin, 0, page_len) + r * CODE
        code = jnp.where(table_ref[r : r + 1, :] == slot, live, code)
    code_ref[...] = jnp.sum(code.astype(jnp.float32).T, axis=0, keepdims=True).astype(jnp.int32)
    early.wait()


def attend_kernel(
    code_ref, q_ref, early_ref, k_hbm, v_hbm, out_ref, k_ref, v_ref, s_ref, mx_ref, sum_ref, acc_ref, sems
):
    pages, page_len, head_dim = v_ref.shape
    requests, group, _ = q_ref.shape
    early = early_ref.shape[0]
    factor = head_dim ** (-0.5) * LOG2E
    late = pltpu.make_async_copy(k_hbm.at[pl.ds(early, pages - early)], k_ref, sems.at[0])
    late.start()
    step = pages // CHUNKS
    blocks = [
        pltpu.make_async_copy(v_hbm.at[pl.ds(i * step, step)], v_ref.at[pl.ds(i * step, step)], sems.at[1 + i])
        for i in range(CHUNKS)
    ]
    for block in blocks:
        block.start()
    token = lax.broadcasted_iota(jnp.int32, (group, page_len), 1)
    halves = page_len // head_dim
    mx_ref[...] = jnp.full(mx_ref.shape, EMPTY, jnp.float32)
    sum_ref[...] = jnp.zeros(sum_ref.shape, jnp.float32)
    acc_ref[...] = jnp.zeros(acc_ref.shape, jnp.float32)

    def score(p, key_page):
        code = code_ref[0, p]
        owner = code // CODE
        s = lax.dot_general(
            q_ref[owner], key_page, (((1,), (1,)), ((), ())), preferred_element_type=jnp.float32
        )
        s = jnp.where(token < code % CODE, s, MASKED)
        s_ref[p] = s
        top = s[:, :head_dim]
        for h in range(1, halves):
            top = jnp.maximum(top, s[:, h * head_dim : (h + 1) * head_dim])
        mx_ref[owner] = jnp.maximum(mx_ref[owner], top)

    for p in range(early):
        score(p, early_ref[p])
    late.wait()
    for p in range(early, pages):
        score(p, k_ref[p - early])
    mx_ref[...] = jnp.broadcast_to(jnp.max(mx_ref[...], axis=-1, keepdims=True), mx_ref.shape)

    for i, block in enumerate(blocks):
        block.wait()
        for p in range(i * step, (i + 1) * step):
            owner = code_ref[0, p] // CODE
            top = mx_ref[owner]
            parts = [
                jnp.exp2((s_ref[p, :, h * head_dim : (h + 1) * head_dim] - top) * factor)
                for h in range(halves)
            ]
            sum_ref[owner] += sum(parts)
            weights = jnp.concatenate(parts, axis=1).astype(jnp.bfloat16)
            acc_ref[owner] += jnp.dot(weights, v_ref[p], preferred_element_type=jnp.float32)

    out_ref[:, :group, :] = acc_ref[...].astype(jnp.bfloat16)
    total = jnp.broadcast_to(jnp.sum(sum_ref[...], axis=-1, keepdims=True), sum_ref.shape)
    lane = lax.broadcasted_iota(jnp.int32, sum_ref.shape, 2)
    row = lax.broadcasted_iota(jnp.int32, sum_ref.shape, 1)
    stats = jnp.zeros(sum_ref.shape, jnp.float32)
    for k, part in enumerate(three_parts(mx_ref[...]) + three_parts(total)):
        stats = jnp.where(lane == row + k * group, part, stats)
    stats = jnp.sum(stats, axis=1, keepdims=True)
    out_ref[:, group:, :] = jnp.broadcast_to(stats, (requests, STAT_ROWS, head_dim)).astype(jnp.bfloat16)


def join_kernel(parts_ref, out_ref):
    sources, rows, head_dim = parts_ref.shape
    group = rows - STAT_ROWS
    factor = head_dim ** (-0.5) * LOG2E
    stats = parts_ref[:, group:, :].astype(jnp.float32)[:, 0, :]
    peak = stats[:, :group] + stats[:, group : 2 * group] + stats[:, 2 * group : 3 * group]
    total = (
        stats[:, 3 * group : 4 * group] + stats[:, 4 * group : 5 * group] + stats[:, 5 * group : 6 * group]
    )
    weight = jnp.exp2((peak - jnp.max(peak, axis=0, keepdims=True)) * factor)
    weight = weight / jnp.sum(weight * total, axis=0, keepdims=True)
    weight = weight.T
    result = jnp.zeros((group, head_dim), jnp.float32)
    for s in range(sources):
        result += weight[:, s : s + 1] * parts_ref[s, :group, :].astype(jnp.float32)
    for g in range(group):
        out_ref[0, :, g * head_dim : (g + 1) * head_dim] = result[g : g + 1, :].astype(jnp.bfloat16)


def per_device(queries, keys, values, page_table, lengths):
    pages, _, page_len, head_dim = keys.shape
    group = queries.shape[2] // head_dim
    requests = page_table.shape[0]
    vmem = pl.BlockSpec(memory_space=pltpu.VMEM)
    smem = pl.BlockSpec(memory_space=pltpu.SMEM)
    hbm = pl.BlockSpec(memory_space=pltpu.HBM)

    def stay(array):
        return pltpu.with_memory_space_constraint(array, pltpu.HBM)

    key_pages = keys.reshape(pages, page_len, head_dim)
    value_pages = values.reshape(pages, page_len, head_dim)
    spread = pl.pallas_call(
        spread_kernel,
        out_shape=jax.ShapeDtypeStruct((requests, group, head_dim), jnp.bfloat16),
        in_specs=[hbm],
        out_specs=vmem,
        scratch_shapes=[pltpu.VMEM(queries.shape, queries.dtype), pltpu.SemaphoreType.DMA],
        compiler_params=pltpu.CompilerParams(vmem_limit_bytes=4 * MIB),
    )(stay(queries))
    query_all = lax.all_to_all(spread, "pool", 0, 0, tiled=True)
    code, early = pl.pallas_call(
        prepare_kernel,
        out_shape=[
            jax.ShapeDtypeStruct((1, pages), jnp.int32),
            pltpu.VMEM((EARLY, page_len, head_dim), jnp.bfloat16),
        ],
        in_specs=[hbm, hbm, hbm],
        out_specs=[vmem, vmem],
        scratch_shapes=[
            pltpu.SMEM(lengths.shape, jnp.int32),
            pltpu.VMEM(page_table.shape, jnp.int32),
            pltpu.SemaphoreType.DMA((3,)),
        ],
        compiler_params=pltpu.CompilerParams(vmem_limit_bytes=8 * MIB),
        cost_estimate=pl.CostEstimate(
            flops=10**6, bytes_accessed=2 * EARLY * page_len * head_dim, transcendentals=0
        ),
    )(stay(lengths), stay(page_table), stay(key_pages))
    partial = pl.pallas_call(
        attend_kernel,
        out_shape=jax.ShapeDtypeStruct((requests, group + STAT_ROWS, head_dim), jnp.bfloat16),
        in_specs=[smem, vmem, vmem, hbm, hbm],
        out_specs=vmem,
        scratch_shapes=[
            pltpu.VMEM((pages - EARLY, page_len, head_dim), jnp.bfloat16),
            pltpu.VMEM((pages, page_len, head_dim), jnp.bfloat16),
            pltpu.VMEM((pages, group, page_len), jnp.float32),
            pltpu.VMEM((requests, group, head_dim), jnp.float32),
            pltpu.VMEM((requests, group, head_dim), jnp.float32),
            pltpu.VMEM((requests, group, head_dim), jnp.float32),
            pltpu.SemaphoreType.DMA((1 + CHUNKS,)),
        ],
        compiler_params=pltpu.CompilerParams(vmem_limit_bytes=24 * MIB),
    )(code, query_all, early, stay(key_pages), stay(value_pages))
    received = lax.all_to_all(partial, "pool", 0, 0, tiled=True)
    return pl.pallas_call(
        join_kernel,
        out_shape=jax.ShapeDtypeStruct((1, 1, group * head_dim), jnp.bfloat16),
        in_specs=[vmem],
        out_specs=vmem,
        compiler_params=pltpu.CompilerParams(vmem_limit_bytes=4 * MIB),
    )(received)


def solution(mesh):
    placed = (
        P("pool", "head", None),
        P("pool", "head", None, None),
        P("pool", "head", None, None),
        P(),
        P(),
    )
    return jax.shard_map(
        per_device, mesh=mesh, in_specs=placed, out_specs=P("pool", "head", None), check_vma=False
    )
```

time: 41 us -> 35.3 us (0.86)
  local copies, waits for them, and re-layouts: 5.03 us -> 0 us
  other arithmetic: 2.86 us -> 0 us
  Pallas kernels: 6.59 us -> 8.83 us
    unnamed x4 -> x0, local copies, waits for them, and re-layouts: 4.38 us -> none
    pallas_call x1 -> x3, Pallas kernels: 1.99 us -> 4.37 us  [the longest x1 1.94 us: per_device(): pl.pallas_call(prepare_kernel, out_shape=[jax.ShapeDtypeStruct((1, pages)...]
    reduce_sum x1 -> x0, other arithmetic: 1.4 us -> none  [per_device(): live = jnp.sum(jnp.where(match, left[:, :, None], 0), axis=(0, 1))]
    sub x1 -> x0, other arithmetic: 0.73 us -> none  [per_device(): lengths[:, None]]
    unnamed x1 -> x0, other arithmetic: 0.73 us -> none
    broadcast_in_dim x1 -> x0, local copies, waits for them, and re-layouts: 0.66 us -> none  [per_device(): jnp.broadcast_to(queries.reshape(1, group, head_dim), (requests, group, h...]
  transfers between devices with their start and end apart: 1 -> 1, of which waited for: 1 -> 1; matrix products, arithmetic and copies ran while one was open for 5% -> 0% of each run, Pallas kernels for 0% -> 6%
where the time goes in v2:
time: 35.3 us; the launch traced here: 35.1 us
  blocking collectives  11.9 us (34%)
  Pallas kernels  8.83 us (25%)
  starting transfers between devices  8.6 us (24%)
  waiting for transfers between devices  5.68 us (16%)
    all_to_all x1, blocking collectives, per_device(): received = lax.all_to_all(partial, 'pool', 0, 0, tiled=True)  11.9 us
    all_to_all x1, starting transfers between devices, per_device(): query_all = lax.all_to_all(spread, 'pool', 0, 0, tiled=True)  8.6 us
    all_to_all x1, waiting for transfers between devices, per_device(): query_all = lax.all_to_all(spread, 'pool', 0, 0, tiled=True)  5.68 us
    pallas_call x1, Pallas kernels, per_device(): pl.pallas_call(attend_kernel, out_shape=jax.ShapeDtypeStruct((requests, g...  4.46 us
    pallas_call x1, Pallas kernels, per_device(): pl.pallas_call(prepare_kernel, out_shape=[jax.ShapeDtypeStruct((1, pages)...  1.94 us
    pallas_call x1, Pallas kernels, per_device(): pl.pallas_call(spread_kernel, out_shape=jax.ShapeDtypeStruct((requests, g...  1.37 us
    pallas_call x1, Pallas kernels, per_device(): pl.pallas_call(join_kernel, out_shape=jax.ShapeDtypeStruct((1, 1, group *...  1.07 us
  transfers between devices with their start and end apart: 1, of which 1 were waited for; matrix products, arithmetic and copies ran while one was open for 0% of the time, Pallas kernels for 6%

profile of v2, /device:TPU:1, one launch (start us, length us, event | category | flops | bytes accessed | tf_op | source)
XLA Modules:
  0.0 35.1 jit_solution(13815386384505415112)
XLA Ops:
  0.0 1.4 %shard_map.56 = bf16[32,16,128]{2,1,0:T(8,128)(2,1)} custom-call(bf16[1,1,2048]{2,1,0:T(2,128)(2,1)} %q_hbm.1), custom_call_target="tpu_custom_call" | custom-call | tf_op jit(solution)/shard_map/pallas_call | solution.py:154
  1.4 8.6 %all-to-all-start = ((bf16[32,16,128]{2,1,0:T(8,128)(2,1)}), bf16[32,16,128]{2,1,0:T(8,128)(2,1)S(1)}, u32[]{:S(2)}, u32[]{:S(2)}) async-start(bf16[32,16,128]{2,1,0:T(8,128)(2,1)} %shard_map.56), calls=%async_computation | async-start | bytes 262144 | tf_op jit(solution)/shard_map/all_to_all | solution.py:162
  10.0 1.9 %shard_map.55 = (s32[1,64]{1,0:T(1,128)S(1)}, bf16[48,256,128]{2,1,0:T(8,128)(2,1)S(1)}) custom-call(s32[32]{0:T(128)} %length_hbm.1, s32[32,64]{1,0:T(8,128)} %table_hbm.1, bf16[64,256,128]{2,1,0:T(8,128)(2,1)} %bitcast.2), custom_call_target="tpu_custom_call" | custom-call | flops 1000000 | bytes 3145728 | tf_op jit(solution)/shard_map/pallas_call | solution.py:163
  11.9 5.7 %all-to-all-done.q_ref = bf16[32,16,128]{2,1,0:T(8,128)(2,1)S(1)} async-done(((bf16[32,16,128]{2,1,0:T(8,128)(2,1)}), bf16[32,16,128]{2,1,0:T(8,128)(2,1)S(1)}, u32[]{:S(2)}, u32[]{:S(2)}) %all-to-all-start) | async-done | bytes 131104 | tf_op jit(solution)/shard_map/all_to_all | solution.py:162
  17.6 4.5 %shard_map.57 = bf16[32,24,128]{2,1,0:T(8,128)(2,1)S(1)} custom-call(s32[1,64]{1,0:T(1,128)S(1)} %get-tuple-element.7.code_ref, bf16[32,16,128]{2,1,0:T(8,128)(2,1)S(1)} %all-to-all-done.q_ref, bf16[48,256,128]{2,1,0:T(8,128)(2,1)S(1)} %get-tuple-element.8.early_ref, bf16[64,256,128]{2,1,0:T(8,128)(2,1)} %bitcast.3, bf16[64,256,128]{2,1,0:T(8,128)(2,1)} %bitcast.4), custom_call_target="tpu_custom_call" | custom-call | tf_op jit(solution)/shard_map/pallas_call | solution.py:181
  22.1 11.9 %all_to_all.10.parts_ref = bf16[32,24,128]{2,1,0:T(8,128)(2,1)S(1)} all-to-all(bf16[32,24,128]{2,1,0:T(8,128)(2,1)S(1)} %shard_map.57), channel_id=1, replica_groups=mesh['pool'=32,'head'=8] {'pool'}, dimensions={0} | all-to-all | bytes 393216 | tf_op jit(solution)/shard_map/all_to_all | solution.py:197
  34.0 1.1 %shard_map.58 = bf16[1,1,2048]{2,1,0:T(2,128)(2,1)} custom-call(bf16[32,24,128]{2,1,0:T(8,128)(2,1)S(1)} %all_to_all.10.parts_ref), custom_call_target="tpu_custom_call" | custom-call | tf_op jit(solution)/shard_map/pallas_call | solution.py:198
Async XLA Ops:
  1.4 16.2 %all-to-all-start = ((bf16[32,16,128]{2,1,0:T(8,128)(2,1)}), bf16[32,16,128]{2,1,0:T(8,128)(2,1)S(1)}, u32[]{:S(2)}, u32[]{:S(2)}) async-start(bf16[32,16,128]{2,1,0:T(8,128)(2,1)} %shard_map.56), calls=%async_computation | async-start | bytes 262144 | tf_op jit(solution)/shard_map/all_to_all | solution.py:162

commit v3 on v2

--- a/solution.py
+++ b/solution.py
@@ -54,12 +54,14 @@
 
 
 def attend_kernel(
-    code_ref, q_ref, early_ref, k_hbm, v_hbm, out_ref, k_ref, v_ref, s_ref, mx_ref, sum_ref, acc_ref, sems
+    code_vmem, q_ref, early_ref, k_hbm, v_hbm, out_ref, code_ref, k_ref, v_ref, s_ref, mx_ref, sum_ref, acc_ref, sems
 ):
     pages, page_len, head_dim = v_ref.shape
     requests, group, _ = q_ref.shape
     early = early_ref.shape[0]
     factor = head_dim ** (-0.5) * LOG2E
+    codes = pltpu.make_async_copy(code_vmem, code_ref, sems.at[1 + CHUNKS])
+    codes.start()
     late = pltpu.make_async_copy(k_hbm.at[pl.ds(early, pages - early)], k_ref, sems.at[0])
     late.start()
     step = pages // CHUNKS
@@ -74,6 +76,8 @@
     mx_ref[...] = jnp.full(mx_ref.shape, EMPTY, jnp.float32)
     sum_ref[...] = jnp.zeros(sum_ref.shape, jnp.float32)
     acc_ref[...] = jnp.zeros(acc_ref.shape, jnp.float32)
+
+    codes.wait()
 
     def score(p, key_page):
         code = code_ref[0, p]
@@ -143,7 +147,6 @@
     group = queries.shape[2] // head_dim
     requests = page_table.shape[0]
     vmem = pl.BlockSpec(memory_space=pltpu.VMEM)
-    smem = pl.BlockSpec(memory_space=pltpu.SMEM)
     hbm = pl.BlockSpec(memory_space=pltpu.HBM)
 
     def stay(array):
@@ -181,16 +184,17 @@
     partial = pl.pallas_call(
         attend_kernel,
         out_shape=jax.ShapeDtypeStruct((requests, group + STAT_ROWS, head_dim), jnp.bfloat16),
-        in_specs=[smem, vmem, vmem, hbm, hbm],
+        in_specs=[vmem, vmem, vmem, hbm, hbm],
         out_specs=vmem,
         scratch_shapes=[
+            pltpu.SMEM((1, pages), jnp.int32),
             pltpu.VMEM((pages - EARLY, page_len, head_dim), jnp.bfloat16),
             pltpu.VMEM((pages, page_len, head_dim), jnp.bfloat16),
             pltpu.VMEM((pages, group, page_len), jnp.float32),
             pltpu.VMEM((requests, group, head_dim), jnp.float32),
             pltpu.VMEM((requests, group, head_dim), jnp.float32),
             pltpu.VMEM((requests, group, head_dim), jnp.float32),
-            pltpu.SemaphoreType.DMA((1 + CHUNKS,)),
+            pltpu.SemaphoreType.DMA((2 + CHUNKS,)),
         ],
         compiler_params=pltpu.CompilerParams(vmem_limit_bytes=24 * MIB),
     )(code, query_all, early, stay(key_pages), stay(value_pages))

time: 35.3 us -> 34 us (0.963)
  Pallas kernels: 8.83 us -> 7.52 us
    pallas_call x1, Pallas kernels: 4.46 us -> 3.14 us  [per_device(): pl.pallas_call(attend_kernel, out_shape=jax.ShapeDtypeStruct((requests, g...]
where the time goes in v3:
time: 34 us; the launch traced here: 33.8 us
  blocking collectives  11.9 us (35%)
  starting transfers between devices  8.6 us (25%)
  Pallas kernels  7.52 us (22%)
  waiting for transfers between devices  5.68 us (17%)
    all_to_all x1, blocking collectives, per_device(): received = lax.all_to_all(partial, 'pool', 0, 0, tiled=True)  11.9 us
    all_to_all x1, starting transfers between devices, per_device(): query_all = lax.all_to_all(spread, 'pool', 0, 0, tiled=True)  8.6 us
    all_to_all x1, waiting for transfers between devices, per_device(): query_all = lax.all_to_all(spread, 'pool', 0, 0, tiled=True)  5.68 us
    pallas_call x1, Pallas kernels, per_device(): pl.pallas_call(attend_kernel, out_shape=jax.ShapeDtypeStruct((requests, g...  3.14 us
    pallas_call x1, Pallas kernels, per_device(): pl.pallas_call(prepare_kernel, out_shape=[jax.ShapeDtypeStruct((1, pages)...  1.94 us
    pallas_call x1, Pallas kernels, per_device(): pl.pallas_call(spread_kernel, out_shape=jax.ShapeDtypeStruct((requests, g...  1.37 us
    pallas_call x1, Pallas kernels, per_device(): pl.pallas_call(join_kernel, out_shape=jax.ShapeDtypeStruct((1, 1, group *...  1.07 us
  transfers between devices with their start and end apart: 1, of which 1 were waited for; matrix products, arithmetic and copies ran while one was open for 0% of the time, Pallas kernels for 6%

profile of v3, /device:TPU:1, one launch (start us, length us, event | category | flops | bytes accessed | tf_op | source)
XLA Modules:
  0.0 33.8 jit_solution(256998311233556223)
XLA Ops:
  0.0 1.4 %shard_map.56 = bf16[32,16,128]{2,1,0:T(8,128)(2,1)} custom-call(bf16[1,1,2048]{2,1,0:T(2,128)(2,1)} %q_hbm.1), custom_call_target="tpu_custom_call" | custom-call | tf_op jit(solution)/shard_map/pallas_call | solution.py:157
  1.4 8.6 %all-to-all-start = ((bf16[32,16,128]{2,1,0:T(8,128)(2,1)}), bf16[32,16,128]{2,1,0:T(8,128)(2,1)S(1)}, u32[]{:S(2)}, u32[]{:S(2)}) async-start(bf16[32,16,128]{2,1,0:T(8,128)(2,1)} %shard_map.56), calls=%async_computation | async-start | bytes 262144 | tf_op jit(solution)/shard_map/all_to_all | solution.py:165
  10.0 1.9 %shard_map.55 = (s32[1,64]{1,0:T(1,128)S(1)}, bf16[48,256,128]{2,1,0:T(8,128)(2,1)S(1)}) custom-call(s32[32]{0:T(128)} %length_hbm.1, s32[32,64]{1,0:T(8,128)} %table_hbm.1, bf16[64,256,128]{2,1,0:T(8,128)(2,1)} %bitcast.2), custom_call_target="tpu_custom_call" | custom-call | flops 1000000 | bytes 3145728 | tf_op jit(solution)/shard_map/pallas_call | solution.py:166
  11.9 5.7 %all-to-all-done.q_ref = bf16[32,16,128]{2,1,0:T(8,128)(2,1)S(1)} async-done(((bf16[32,16,128]{2,1,0:T(8,128)(2,1)}), bf16[32,16,128]{2,1,0:T(8,128)(2,1)S(1)}, u32[]{:S(2)}, u32[]{:S(2)}) %all-to-all-start) | async-done | bytes 131104 | tf_op jit(solution)/shard_map/all_to_all | solution.py:165
  17.6 3.1 %shard_map.57 = bf16[32,24,128]{2,1,0:T(8,128)(2,1)S(1)} custom-call(s32[1,64]{1,0:T(1,128)S(1)} %get-tuple-element.7.code_vmem, bf16[32,16,128]{2,1,0:T(8,128)(2,1)S(1)} %all-to-all-done.q_ref, bf16[48,256,128]{2,1,0:T(8,128)(2,1)S(1)} %get-tuple-element.8.early_ref, bf16[64,256,128]{2,1,0:T(8,128)(2,1)} %bitcast.3, bf16[64,256,128]{2,1,0:T(8,128)(2,1)} %bitcast.4), custom_call_target="tpu_custom_call" | custom-call | tf_op jit(solution)/shard_map/pallas_call | solution.py:184
  20.8 11.9 %all_to_all.10.parts_ref = bf16[32,24,128]{2,1,0:T(8,128)(2,1)S(1)} all-to-all(bf16[32,24,128]{2,1,0:T(8,128)(2,1)S(1)} %shard_map.57), channel_id=1, replica_groups=mesh['pool'=32,'head'=8] {'pool'}, dimensions={0} | all-to-all | bytes 393216 | tf_op jit(solution)/shard_map/all_to_all | solution.py:201
  32.7 1.1 %shard_map.58 = bf16[1,1,2048]{2,1,0:T(2,128)(2,1)} custom-call(bf16[32,24,128]{2,1,0:T(8,128)(2,1)S(1)} %all_to_all.10.parts_ref), custom_call_target="tpu_custom_call" | custom-call | tf_op jit(solution)/shard_map/pallas_call | solution.py:202
Async XLA Ops:
  1.4 16.2 %all-to-all-start = ((bf16[32,16,128]{2,1,0:T(8,128)(2,1)}), bf16[32,16,128]{2,1,0:T(8,128)(2,1)S(1)}, u32[]{:S(2)}, u32[]{:S(2)}) async-start(bf16[32,16,128]{2,1,0:T(8,128)(2,1)} %shard_map.56), calls=%async_computation | async-start | bytes 262144 | tf_op jit(solution)/shard_map/all_to_all | solution.py:165

commit v4 on v2

--- a/solution.py
+++ b/solution.py
@@ -9,8 +9,8 @@
 EMPTY = -1.5e38
 STAT_ROWS = 8
 CODE = 512
-EARLY = 48
-CHUNKS = 2
+EARLY = 50
+BLOCKS = (0, 32, 52, 64)
 MIB = 1024 * 1024
 LOG2E = 1.4426950408889634
 
@@ -32,7 +32,7 @@
     out_ref[...] = jnp.broadcast_to(tile[None], out_ref.shape)
 
 
-def prepare_kernel(length_hbm, table_hbm, k_hbm, code_ref, early_ref, length_ref, table_ref, sems):
+def prepare_kernel(length_hbm, table_hbm, k_hbm, code_ref, early_ref, length_ref, table_ref, row_ref, sems):
     pages, page_len, _ = k_hbm.shape
     requests, most_pages = table_ref.shape
     lengths = pltpu.make_async_copy(length_hbm, length_ref, sems.at[0])
@@ -49,7 +49,10 @@
     for r in range(requests):
         live = jnp.clip(length_ref[r] - begin, 0, page_len) + r * CODE
         code = jnp.where(table_ref[r : r + 1, :] == slot, live, code)
-    code_ref[...] = jnp.sum(code.astype(jnp.float32).T, axis=0, keepdims=True).astype(jnp.int32)
+    row_ref[...] = jnp.sum(code.astype(jnp.float32).T, axis=0, keepdims=True).astype(jnp.int32)
+    codes = pltpu.make_async_copy(row_ref, code_ref, sems.at[3])
+    codes.start()
+    codes.wait()
     early.wait()
 
 
@@ -62,18 +65,21 @@
     factor = head_dim ** (-0.5) * LOG2E
     late = pltpu.make_async_copy(k_hbm.at[pl.ds(early, pages - early)], k_ref, sems.at[0])
     late.start()
-    step = pages // CHUNKS
+    bounds = list(zip(BLOCKS, BLOCKS[1:]))
     blocks = [
-        pltpu.make_async_copy(v_hbm.at[pl.ds(i * step, step)], v_ref.at[pl.ds(i * step, step)], sems.at[1 + i])
-        for i in range(CHUNKS)
+        pltpu.make_async_copy(v_hbm.at[pl.ds(lo, hi - lo)], v_ref.at[pl.ds(lo, hi - lo)], sems.at[2 + i])
+        for i, (lo, hi) in enumerate(bounds)
     ]
     for block in blocks:
         block.start()
     token = lax.broadcasted_iota(jnp.int32, (group, page_len), 1)
     halves = page_len // head_dim
-    mx_ref[...] = jnp.full(mx_ref.shape, EMPTY, jnp.float32)
-    sum_ref[...] = jnp.zeros(sum_ref.shape, jnp.float32)
-    acc_ref[...] = jnp.zeros(acc_ref.shape, jnp.float32)
+
+    @pl.when(code_ref[0, 0] >= 0)
+    def _():
+        mx_ref[...] = jnp.full(mx_ref.shape, EMPTY, jnp.float32)
+        sum_ref[...] = jnp.zeros(sum_ref.shape, jnp.float32)
+        acc_ref[...] = jnp.zeros(acc_ref.shape, jnp.float32)
 
     def score(p, key_page):
         code = code_ref[0, p]
@@ -95,9 +101,9 @@
         score(p, k_ref[p - early])
     mx_ref[...] = jnp.broadcast_to(jnp.max(mx_ref[...], axis=-1, keepdims=True), mx_ref.shape)
 
-    for i, block in enumerate(blocks):
+    for block, (lo, hi) in zip(blocks, bounds):
         block.wait()
-        for p in range(i * step, (i + 1) * step):
+        for p in range(lo, hi):
             owner = code_ref[0, p] // CODE
             top = mx_ref[owner]
             parts = [
@@ -123,17 +129,24 @@
     sources, rows, head_dim = parts_ref.shape
     group = rows - STAT_ROWS
     factor = head_dim ** (-0.5) * LOG2E
-    stats = parts_ref[:, group:, :].astype(jnp.float32)[:, 0, :]
-    peak = stats[:, :group] + stats[:, group : 2 * group] + stats[:, 2 * group : 3 * group]
-    total = (
-        stats[:, 3 * group : 4 * group] + stats[:, 4 * group : 5 * group] + stats[:, 5 * group : 6 * group]
-    )
-    weight = jnp.exp2((peak - jnp.max(peak, axis=0, keepdims=True)) * factor)
-    weight = weight / jnp.sum(weight * total, axis=0, keepdims=True)
-    weight = weight.T
-    result = jnp.zeros((group, head_dim), jnp.float32)
+    tiles = parts_ref[:, group:, :].astype(jnp.float32)
+    place = lax.broadcasted_iota(jnp.int32, (STAT_ROWS, head_dim), 0)
+    blocks = []
+    for first in range(0, sources, STAT_ROWS):
+        block = tiles[first]
+        for k in range(1, STAT_ROWS):
+            block = jnp.where(place == k, tiles[first + k], block)
+        blocks.append(block)
+    stats = jnp.concatenate(blocks, axis=0).T
+    part = [stats[k * group : (k + 1) * group, :] for k in range(6)]
+    peak = part[0] + part[1] + part[2]
+    total = part[3] + part[4] + part[5]
+    weight = jnp.exp2((peak - jnp.max(peak, axis=1, keepdims=True)) * factor)
+    whole = jnp.sum(weight * total, axis=1, keepdims=True)
+    sums = [jnp.zeros((group, head_dim), jnp.float32) for _ in range(4)]
     for s in range(sources):
-        result += weight[:, s : s + 1] * parts_ref[s, :group, :].astype(jnp.float32)
+        sums[s % 4] += weight[:, s : s + 1] * parts_ref[s, :group, :].astype(jnp.float32)
+    result = ((sums[0] + sums[1]) + (sums[2] + sums[3])) / whole
     for g in range(group):
         out_ref[0, :, g * head_dim : (g + 1) * head_dim] = result[g : g + 1, :].astype(jnp.bfloat16)
 
@@ -143,8 +156,8 @@
     group = queries.shape[2] // head_dim
     requests = page_table.shape[0]
     vmem = pl.BlockSpec(memory_space=pltpu.VMEM)
+    hbm = pl.BlockSpec(memory_space=pltpu.HBM)
     smem = pl.BlockSpec(memory_space=pltpu.SMEM)
-    hbm = pl.BlockSpec(memory_space=pltpu.HBM)
 
     def stay(array):
         return pltpu.with_memory_space_constraint(array, pltpu.HBM)
@@ -163,15 +176,16 @@
     code, early = pl.pallas_call(
         prepare_kernel,
         out_shape=[
-            jax.ShapeDtypeStruct((1, pages), jnp.int32),
+            pltpu.SMEM((1, pages), jnp.int32),
             pltpu.VMEM((EARLY, page_len, head_dim), jnp.bfloat16),
         ],
         in_specs=[hbm, hbm, hbm],
-        out_specs=[vmem, vmem],
+        out_specs=[smem, vmem],
         scratch_shapes=[
             pltpu.SMEM(lengths.shape, jnp.int32),
             pltpu.VMEM(page_table.shape, jnp.int32),
-            pltpu.SemaphoreType.DMA((3,)),
+            pltpu.VMEM((1, pages), jnp.int32),
+            pltpu.SemaphoreType.DMA((4,)),
         ],
         compiler_params=pltpu.CompilerParams(vmem_limit_bytes=8 * MIB),
         cost_estimate=pl.CostEstimate(
@@ -190,10 +204,10 @@
             pltpu.VMEM((requests, group, head_dim), jnp.float32),
             pltpu.VMEM((requests, group, head_dim), jnp.float32),
             pltpu.VMEM((requests, group, head_dim), jnp.float32),
-            pltpu.SemaphoreType.DMA((1 + CHUNKS,)),
+            pltpu.SemaphoreType.DMA((1 + len(BLOCKS),)),
         ],
         compiler_params=pltpu.CompilerParams(vmem_limit_bytes=24 * MIB),
-    )(code, query_all, early, stay(key_pages), stay(value_pages))
+    )(pltpu.with_memory_space_constraint(code, pltpu.SMEM), query_all, early, stay(key_pages), stay(value_pages))
     received = lax.all_to_all(partial, "pool", 0, 0, tiled=True)
     return pl.pallas_call(
         join_kernel,

time: 35.3 us -> 33.9 us (0.960)
  Pallas kernels: 8.83 us -> 7.4 us
    pallas_call x1, Pallas kernels: 4.46 us -> 3.03 us  [per_device(): pl.pallas_call(attend_kernel, out_shape=jax.ShapeDtypeStruct((requests, g...]
where the time goes in v4:
time: 33.9 us; the launch traced here: 33.6 us
  blocking collectives  11.9 us (35%)
  starting transfers between devices  8.6 us (25%)
  Pallas kernels  7.4 us (22%)
  waiting for transfers between devices  5.64 us (17%)
    all_to_all x1, blocking collectives, per_device(): received = lax.all_to_all(partial, 'pool', 0, 0, tiled=True)  11.9 us
    all_to_all x1, starting transfers between devices, per_device(): query_all = lax.all_to_all(spread, 'pool', 0, 0, tiled=True)  8.6 us
    all_to_all x1, waiting for transfers between devices, per_device(): query_all = lax.all_to_all(spread, 'pool', 0, 0, tiled=True)  5.64 us
    pallas_call x1, Pallas kernels, per_device(): pl.pallas_call(attend_kernel, out_shape=jax.ShapeDtypeStruct((requests, g...  3.03 us
    pallas_call x1, Pallas kernels, per_device(): pl.pallas_call(prepare_kernel, out_shape=[pltpu.SMEM((1, pages), jnp.int3...  1.98 us
    pallas_call x1, Pallas kernels, per_device(): pl.pallas_call(spread_kernel, out_shape=jax.ShapeDtypeStruct((requests, g...  1.37 us
    pallas_call x1, Pallas kernels, per_device(): pl.pallas_call(join_kernel, out_shape=jax.ShapeDtypeStruct((1, 1, group *...  1.02 us
  transfers between devices with their start and end apart: 1, of which 1 were waited for; matrix products, arithmetic and copies ran while one was open for 0% of the time, Pallas kernels for 6%

profile of v4, /device:TPU:1, one launch (start us, length us, event | category | flops | bytes accessed | tf_op | source)
XLA Modules:
  0.0 33.6 jit_solution(16723516844124548279)
XLA Ops:
  0.0 1.4 %shard_map.56 = bf16[32,16,128]{2,1,0:T(8,128)(2,1)} custom-call(bf16[1,1,2048]{2,1,0:T(2,128)(2,1)} %q_hbm.1), custom_call_target="tpu_custom_call" | custom-call | tf_op jit(solution)/shard_map/pallas_call | solution.py:167
  1.4 8.6 %all-to-all-start = ((bf16[32,16,128]{2,1,0:T(8,128)(2,1)}), bf16[32,16,128]{2,1,0:T(8,128)(2,1)S(1)}, u32[]{:S(2)}, u32[]{:S(2)}) async-start(bf16[32,16,128]{2,1,0:T(8,128)(2,1)} %shard_map.56), calls=%async_computation | async-start | bytes 262144 | tf_op jit(solution)/shard_map/all_to_all | solution.py:175
  10.0 2.0 %shard_map.55 = (s32[1,64]{1,0:T(1,128)S(4)}, bf16[50,256,128]{2,1,0:T(8,128)(2,1)S(1)}) custom-call(s32[32]{0:T(128)} %length_hbm.1, s32[32,64]{1,0:T(8,128)} %table_hbm.1, bf16[64,256,128]{2,1,0:T(8,128)(2,1)} %bitcast.2), custom_call_target="tpu_custom_call" | custom-call | flops 1000000 | bytes 3276800 | tf_op jit(solution)/shard_map/pallas_call | solution.py:176
  12.0 5.6 %all-to-all-done.q_ref = bf16[32,16,128]{2,1,0:T(8,128)(2,1)S(1)} async-done(((bf16[32,16,128]{2,1,0:T(8,128)(2,1)}), bf16[32,16,128]{2,1,0:T(8,128)(2,1)S(1)}, u32[]{:S(2)}, u32[]{:S(2)}) %all-to-all-start) | async-done | bytes 131104 | tf_op jit(solution)/shard_map/all_to_all | solution.py:175
  17.6 3.0 %shard_map.57 = bf16[32,24,128]{2,1,0:T(8,128)(2,1)S(1)} custom-call(s32[1,64]{1,0:T(1,128)S(4)} %get-tuple-element.7.code_ref, bf16[32,16,128]{2,1,0:T(8,128)(2,1)S(1)} %all-to-all-done.q_ref, bf16[50,256,128]{2,1,0:T(8,128)(2,1)S(1)} %get-tuple-element.8.early_ref, bf16[64,256,128]{2,1,0:T(8,128)(2,1)} %bitcast.3, bf16[64,256,128]{2,1,0:T(8,128)(2,1)} %bitcast.4), custom_call_target="tpu_custom_call" | custom-call | tf_op jit(solution)/shard_map/pallas_call | solution.py:195
  20.6 11.9 %all_to_all.10.parts_ref = bf16[32,24,128]{2,1,0:T(8,128)(2,1)S(1)} all-to-all(bf16[32,24,128]{2,1,0:T(8,128)(2,1)S(1)} %shard_map.57), channel_id=1, replica_groups=mesh['pool'=32,'head'=8] {'pool'}, dimensions={0} | all-to-all | bytes 393216 | tf_op jit(solution)/shard_map/all_to_all | solution.py:211
  32.6 1.0 %shard_map.58 = bf16[1,1,2048]{2,1,0:T(2,128)(2,1)} custom-call(bf16[32,24,128]{2,1,0:T(8,128)(2,1)S(1)} %all_to_all.10.parts_ref), custom_call_target="tpu_custom_call" | custom-call | tf_op jit(solution)/shard_map/pallas_call | solution.py:212
Async XLA Ops:
  1.4 16.2 %all-to-all-start = ((bf16[32,16,128]{2,1,0:T(8,128)(2,1)}), bf16[32,16,128]{2,1,0:T(8,128)(2,1)S(1)}, u32[]{:S(2)}, u32[]{:S(2)}) async-start(bf16[32,16,128]{2,1,0:T(8,128)(2,1)} %shard_map.56), calls=%async_computation | async-start | bytes 262144 | tf_op jit(solution)/shard_map/all_to_all | solution.py:175

commit v5 on v4

v5 whole, which is shorter than its diff:
```python
import jax
import jax.numpy as jnp
from jax import lax
from jax.experimental import pallas as pl
from jax.experimental.pallas import tpu as pltpu
from jax.sharding import PartitionSpec as P

MASKED = -3.0e38
EMPTY = -1.5e38
STAT_ROWS = 8
CODE = 512
PAGE = 256
MIB = 1024 * 1024
LOG2E = 1.4426950408889634


def three_parts(x):
    high = x.astype(jnp.bfloat16).astype(jnp.float32)
    rest = x - high
    middle = rest.astype(jnp.bfloat16).astype(jnp.float32)
    return high, middle, rest - middle


def spread_kernel(q_hbm, length_hbm, table_hbm, out_ref, code_ref, q_ref, length_ref, table_ref, row_ref, sems):
    requests, group, head_dim = out_ref.shape
    pages = code_ref.shape[1]
    most_pages = table_ref.shape[1]
    lengths = pltpu.make_async_copy(length_hbm, length_ref, sems.at[0])
    table = pltpu.make_async_copy(table_hbm, table_ref, sems.at[1])
    query = pltpu.make_async_copy(q_hbm, q_ref, sems.at[2])
    lengths.start()
    table.start()
    query.start()
    lengths.wait()
    table.wait()
    slot = lax.axis_index("pool") * pages + lax.broadcasted_iota(jnp.int32, (pages, most_pages), 0)
    begin = PAGE * lax.broadcasted_iota(jnp.int32, (1, most_pages), 1)
    code = jnp.zeros((pages, most_pages), jnp.int32)
    for r in range(requests):
        live = jnp.clip(length_ref[r] - begin, 0, PAGE) + r * CODE
        code = jnp.where(table_ref[r : r + 1, :] == slot, live, code)
    row_ref[...] = jnp.sum(code.astype(jnp.float32).T, axis=0, keepdims=True).astype(jnp.int32)
    codes = pltpu.make_async_copy(row_ref, code_ref, sems.at[3])
    codes.start()
    query.wait()
    rows = [q_ref[0, :, g * head_dim : (g + 1) * head_dim].astype(jnp.float32) for g in range(group)]
    tile = jnp.concatenate(rows, axis=0).astype(jnp.bfloat16)
    out_ref[...] = jnp.broadcast_to(tile[None], out_ref.shape)
    codes.wait()


def attend_kernel(code_ref, q_ref, k_ref, v_ref, out_ref, s_ref, mx_ref, sum_ref, acc_ref):
    pages, page_len, head_dim = k_ref.shape
    requests, group, _ = q_ref.shape
    factor = head_dim ** (-0.5) * LOG2E
    token = lax.broadcasted_iota(jnp.int32, (group, page_len), 1)
    halves = page_len // head_dim

    mx_ref[...] = jnp.full(mx_ref.shape, EMPTY, jnp.float32)
    sum_ref[...] = jnp.zeros(sum_ref.shape, jnp.float32)
    acc_ref[...] = jnp.zeros(acc_ref.shape, jnp.float32)

    def score(p, key_page):
        code = code_ref[0, p]
        owner = code // CODE
        s = lax.dot_general(
            q_ref[owner], key_page, (((1,), (1,)), ((), ())), preferred_element_type=jnp.float32
        )
        s = jnp.where(token < code % CODE, s, MASKED)
        s_ref[p] = s
        top = s[:, :head_dim]
        for h in range(1, halves):
            top = jnp.maximum(top, s[:, h * head_dim : (h + 1) * head_dim])
        mx_ref[owner] = jnp.maximum(mx_ref[owner], top)

    for p in range(pages):
        score(p, k_ref[p])
    mx_ref[...] = jnp.broadcast_to(jnp.max(mx_ref[...], axis=-1, keepdims=True), mx_ref.shape)

    for p in range(pages):
        owner = code_ref[0, p] // CODE
        top = mx_ref[owner]
        parts = [
            jnp.exp2((s_ref[p, :, h * head_dim : (h + 1) * head_dim] - top) * factor)
            for h in range(halves)
        ]
        sum_ref[owner] += sum(parts)
        weights = jnp.concatenate(parts, axis=1).astype(jnp.bfloat16)
        acc_ref[owner] += jnp.dot(weights, v_ref[p], preferred_element_type=jnp.float32)

    out_ref[:, :group, :] = acc_ref[...].astype(jnp.bfloat16)
    total = jnp.broadcast_to(jnp.sum(sum_ref[...], axis=-1, keepdims=True), sum_ref.shape)
    lane = lax.broadcasted_iota(jnp.int32, sum_ref.shape, 2)
    row = lax.broadcasted_iota(jnp.int32, sum_ref.shape, 1)
    stats = jnp.zeros(sum_ref.shape, jnp.float32)
    for k, part in enumerate(three_parts(mx_ref[...]) + three_parts(total)):
        stats = jnp.where(lane == row + k * group, part, stats)
    stats = jnp.sum(stats, axis=1, keepdims=True)
    out_ref[:, group:, :] = jnp.broadcast_to(stats, (requests, STAT_ROWS, head_dim)).astype(jnp.bfloat16)


def join_kernel(parts_ref, out_ref):
    sources, rows, head_dim = parts_ref.shape
    group = rows - STAT_ROWS
    factor = head_dim ** (-0.5) * LOG2E
    tiles = parts_ref[:, group:, :].astype(jnp.float32)
    place = lax.broadcasted_iota(jnp.int32, (STAT_ROWS, head_dim), 0)
    blocks = []
    for first in range(0, sources, STAT_ROWS):
        block = tiles[first]
        for k in range(1, STAT_ROWS):
            block = jnp.where(place == k, tiles[first + k], block)
        blocks.append(block)
    stats = jnp.concatenate(blocks, axis=0).T
    part = [stats[k * group : (k + 1) * group, :] for k in range(6)]
    peak = part[0] + part[1] + part[2]
    total = part[3] + part[4] + part[5]
    weight = jnp.exp2((peak - jnp.max(peak, axis=1, keepdims=True)) * factor)
    whole = jnp.sum(weight * total, axis=1, keepdims=True)
    sums = [jnp.zeros((group, head_dim), jnp.float32) for _ in range(4)]
    for s in range(sources):
        sums[s % 4] += weight[:, s : s + 1] * parts_ref[s, :group, :].astype(jnp.float32)
    result = ((sums[0] + sums[1]) + (sums[2] + sums[3])) / whole
    for g in range(group):
        out_ref[0, :, g * head_dim : (g + 1) * head_dim] = result[g : g + 1, :].astype(jnp.bfloat16)


def per_device(queries, keys, values, page_table, lengths):
    pages, _, page_len, head_dim = keys.shape
    group = queries.shape[2] // head_dim
    requests = page_table.shape[0]
    vmem = pl.BlockSpec(memory_space=pltpu.VMEM)
    hbm = pl.BlockSpec(memory_space=pltpu.HBM)
    smem = pl.BlockSpec(memory_space=pltpu.SMEM)

    def stay(array):
        return pltpu.with_memory_space_constraint(array, pltpu.HBM)

    key_pages = keys.reshape(pages, page_len, head_dim)
    value_pages = values.reshape(pages, page_len, head_dim)
    spread, code = pl.pallas_call(
        spread_kernel,
        out_shape=[
            jax.ShapeDtypeStruct((requests, group, head_dim), jnp.bfloat16),
            pltpu.SMEM((1, pages), jnp.int32),
        ],
        in_specs=[hbm, hbm, hbm],
        out_specs=[vmem, smem],
        scratch_shapes=[
            pltpu.VMEM(queries.shape, queries.dtype),
            pltpu.SMEM(lengths.shape, jnp.int32),
            pltpu.VMEM(page_table.shape, jnp.int32),
            pltpu.VMEM((1, pages), jnp.int32),
            pltpu.SemaphoreType.DMA((4,)),
        ],
        compiler_params=pltpu.CompilerParams(vmem_limit_bytes=4 * MIB),
        cost_estimate=pl.CostEstimate(flops=2 * 10**10, bytes_accessed=64 * MIB, transcendentals=0),
    )(stay(queries), stay(lengths), stay(page_table))
    query_all = lax.all_to_all(spread, "pool", 0, 0, tiled=True)
    partial = pl.pallas_call(
        attend_kernel,
        out_shape=jax.ShapeDtypeStruct((requests, group + STAT_ROWS, head_dim), jnp.bfloat16),
        in_specs=[smem, vmem, vmem, vmem],
        out_specs=vmem,
        scratch_shapes=[
            pltpu.VMEM((pages, group, page_len), jnp.float32),
            pltpu.VMEM((requests, group, head_dim), jnp.float32),
            pltpu.VMEM((requests, group, head_dim), jnp.float32),
            pltpu.VMEM((requests, group, head_dim), jnp.float32),
        ],
        compiler_params=pltpu.CompilerParams(vmem_limit_bytes=24 * MIB),
    )(pltpu.with_memory_space_constraint(code, pltpu.SMEM), query_all, key_pages, value_pages)
    received = lax.all_to_all(partial, "pool", 0, 0, tiled=True)
    return pl.pallas_call(
        join_kernel,
        out_shape=jax.ShapeDtypeStruct((1, 1, group * head_dim), jnp.bfloat16),
        in_specs=[vmem],
        out_specs=vmem,
        compiler_params=pltpu.CompilerParams(vmem_limit_bytes=4 * MIB),
    )(received)


def solution(mesh):
    placed = (
        P("pool", "head", None),
        P("pool", "head", None, None),
        P("pool", "head", None, None),
        P(),
        P(),
    )
    return jax.shard_map(
        per_device, mesh=mesh, in_specs=placed, out_specs=P("pool", "head", None), check_vma=False
    )
```

time: 33.9 us -> 33.4 us (0.985)
  blocking collectives: 11.9 us -> 28.2 us
  starting transfers between devices: 8.6 us -> 0 us
  waiting for transfers between devices: 5.64 us -> 0 us
  Pallas kernels: 7.4 us -> 4.95 us
    all_to_all x0 -> x1, blocking collectives: none -> 16.3 us  [per_device(): query_all = lax.all_to_all(spread, 'pool', 0, 0, tiled=True)]
    all_to_all x1 -> x0, starting transfers between devices: 8.6 us -> none  [per_device(): query_all = lax.all_to_all(spread, 'pool', 0, 0, tiled=True)]
    all_to_all x1 -> x0, waiting for transfers between devices: 5.64 us -> none  [per_device(): query_all = lax.all_to_all(spread, 'pool', 0, 0, tiled=True)]
    pallas_call x2 -> x1, Pallas kernels: 3.35 us -> 1.65 us  [per_device(): pl.pallas_call(spread_kernel, out_shape=[jax.ShapeDtypeStruct((requests,...]
    pallas_call x1, Pallas kernels: 3.03 us -> 2.27 us  [per_device(): pl.pallas_call(attend_kernel, out_shape=jax.ShapeDtypeStruct((requests, g...]
  transfers between devices with their start and end apart: 1 -> 0, of which waited for: 1 -> 0; matrix products, arithmetic and copies ran while one was open for 0% -> 0% of each run, Pallas kernels for 6% -> 0%
where the time goes in v5:
time: 33.4 us; the launch traced here: 33.2 us
  blocking collectives  28.2 us (84%)
  Pallas kernels  4.95 us (15%)
    all_to_all x1, blocking collectives, per_device(): query_all = lax.all_to_all(spread, 'pool', 0, 0, tiled=True)  16.3 us
    all_to_all x1, blocking collectives, per_device(): received = lax.all_to_all(partial, 'pool', 0, 0, tiled=True)  12 us
    pallas_call x1, Pallas kernels, per_device(): pl.pallas_call(attend_kernel, out_shape=jax.ShapeDtypeStruct((requests, g...  2.27 us
    pallas_call x1, Pallas kernels, per_device(): pl.pallas_call(spread_kernel, out_shape=[jax.ShapeDtypeStruct((requests,...  1.65 us
    pallas_call x1, Pallas kernels, per_device(): pl.pallas_call(join_kernel, out_shape=jax.ShapeDtypeStruct((1, 1, group *...  1.02 us

profile of v5, /device:TPU:1, one launch (start us, length us, event | category | flops | bytes accessed | tf_op | source)
XLA Modules:
  0.0 33.2 jit_solution(4702070138565673698)
XLA Ops:
  0.0 0.0 copy-start.1
  0.0 0.0 copy-start
  0.0 1.7 %shard_map.55 = (bf16[32,16,128]{2,1,0:T(8,128)(2,1)S(1)}, s32[1,64]{1,0:T(1,128)S(4)}) custom-call(bf16[1,1,2048]{2,1,0:T(2,128)(2,1)} %q_hbm.1, s32[32]{0:T(128)} %length_hbm.1, s32[32,64]{1,0:T(8,128)} %table_hbm.1), custom_call_target="tpu_custom_call" | custom-call | flops 20000000000 | bytes 67108864 | tf_op jit(solution)/shard_map/pallas_call | solution.py:141
  1.7 16.3 %all_to_all.10.q_ref = bf16[32,16,128]{2,1,0:T(8,128)(2,1)S(1)} all-to-all(bf16[32,16,128]{2,1,0:T(8,128)(2,1)S(1)} %get-tuple-element.8), channel_id=1, replica_groups=mesh['pool'=32,'head'=8] {'pool'}, dimensions={0} | all-to-all | bytes 262144 | tf_op jit(solution)/shard_map/all_to_all | solution.py:159
  17.9 0.0 copy-done.1
  17.9 0.0 copy-done
  18.0 2.3 %shard_map.56 = bf16[32,24,128]{2,1,0:T(8,128)(2,1)S(1)} custom-call(s32[1,64]{1,0:T(1,128)S(4)} %get-tuple-element.7.code_ref, bf16[32,16,128]{2,1,0:T(8,128)(2,1)S(1)} %all_to_all.10.q_ref, bf16[64,256,128]{2,1,0:T(8,128)(2,1)S(1)} %bitcast.2, bf16[64,256,128]{2,1,0:T(8,128)(2,1)S(1)} %bitcast.3), custom_call_target="tpu_custom_call" | custom-call | tf_op jit(solution)/shard_map/pallas_call | solution.py:160
  20.2 12.0 %all_to_all.11.parts_ref = bf16[32,24,128]{2,1,0:T(8,128)(2,1)S(1)} all-to-all(bf16[32,24,128]{2,1,0:T(8,128)(2,1)S(1)} %shard_map.56), channel_id=1, replica_groups=mesh['pool'=32,'head'=8] {'pool'}, dimensions={0} | all-to-all | bytes 393216 | tf_op jit(solution)/shard_map/all_to_all | solution.py:173
  32.2 1.0 %shard_map.57 = bf16[1,1,2048]{2,1,0:T(2,128)(2,1)} custom-call(bf16[32,24,128]{2,1,0:T(8,128)(2,1)S(1)} %all_to_all.11.parts_ref), custom_call_target="tpu_custom_call" | custom-call | tf_op jit(solution)/shard_map/pallas_call | solution.py:174
Async XLA Ops:
  0.0 17.9 %copy-start.1 = (bf16[64,1,256,128]{3,2,1,0:T(8,128)(2,1)S(1)}, bf16[64,1,256,128]{3,2,1,0:T(8,128)(2,1)}, u32[]{:S(2)}) copy-start(bf16[64,1,256,128]{3,2,1,0:T(8,128)(2,1)} %param.7) | copy-start | bytes 12582916
  0.0 17.9 %copy-start = (bf16[64,1,256,128]{3,2,1,0:T(8,128)(2,1)S(1)}, bf16[64,1,256,128]{3,2,1,0:T(8,128)(2,1)}, u32[]{:S(2)}) copy-start(bf16[64,1,256,128]{3,2,1,0:T(8,128)(2,1)} %param.6) | copy-start | bytes 12582916

commit v6 on v5

--- a/solution.py
+++ b/solution.py
@@ -21,7 +21,7 @@
     return high, middle, rest - middle
 
 
-def spread_kernel(q_hbm, length_hbm, table_hbm, out_ref, code_ref, q_ref, length_ref, table_ref, row_ref, sems):
+def spread_kernel(q_hbm, length_hbm, table_hbm, out_ref, code_ref, q_ref, length_ref, table_ref, sems):
     requests, group, head_dim = out_ref.shape
     pages = code_ref.shape[1]
     most_pages = table_ref.shape[1]
@@ -39,20 +39,19 @@
     for r in range(requests):
         live = jnp.clip(length_ref[r] - begin, 0, PAGE) + r * CODE
         code = jnp.where(table_ref[r : r + 1, :] == slot, live, code)
-    row_ref[...] = jnp.sum(code.astype(jnp.float32).T, axis=0, keepdims=True).astype(jnp.int32)
-    codes = pltpu.make_async_copy(row_ref, code_ref, sems.at[3])
-    codes.start()
+    code_ref[...] = jnp.sum(code.astype(jnp.float32).T, axis=0, keepdims=True).astype(jnp.int32)
     query.wait()
     rows = [q_ref[0, :, g * head_dim : (g + 1) * head_dim].astype(jnp.float32) for g in range(group)]
     tile = jnp.concatenate(rows, axis=0).astype(jnp.bfloat16)
     out_ref[...] = jnp.broadcast_to(tile[None], out_ref.shape)
-    codes.wait()
 
 
 def attend_kernel(code_ref, q_ref, k_ref, v_ref, out_ref, s_ref, mx_ref, sum_ref, acc_ref):
     pages, page_len, head_dim = k_ref.shape
     requests, group, _ = q_ref.shape
     factor = head_dim ** (-0.5) * LOG2E
+    listed = code_ref[...]
+    codes = [listed[0, p] for p in range(pages)]
     token = lax.broadcasted_iota(jnp.int32, (group, page_len), 1)
     halves = page_len // head_dim
 
@@ -61,7 +60,7 @@
     acc_ref[...] = jnp.zeros(acc_ref.shape, jnp.float32)
 
     def score(p, key_page):
-        code = code_ref[0, p]
+        code = codes[p]
         owner = code // CODE
         s = lax.dot_general(
             q_ref[owner], key_page, (((1,), (1,)), ((), ())), preferred_element_type=jnp.float32
@@ -78,7 +77,7 @@
     mx_ref[...] = jnp.broadcast_to(jnp.max(mx_ref[...], axis=-1, keepdims=True), mx_ref.shape)
 
     for p in range(pages):
-        owner = code_ref[0, p] // CODE
+        owner = codes[p] // CODE
         top = mx_ref[owner]
         parts = [
             jnp.exp2((s_ref[p, :, h * head_dim : (h + 1) * head_dim] - top) * factor)
@@ -131,7 +130,6 @@
     requests = page_table.shape[0]
     vmem = pl.BlockSpec(memory_space=pltpu.VMEM)
     hbm = pl.BlockSpec(memory_space=pltpu.HBM)
-    smem = pl.BlockSpec(memory_space=pltpu.SMEM)
 
     def stay(array):
         return pltpu.with_memory_space_constraint(array, pltpu.HBM)
@@ -142,16 +140,15 @@
         spread_kernel,
         out_shape=[
             jax.ShapeDtypeStruct((requests, group, head_dim), jnp.bfloat16),
-            pltpu.SMEM((1, pages), jnp.int32),
+            jax.ShapeDtypeStruct((1, pages), jnp.int32),
         ],
         in_specs=[hbm, hbm, hbm],
-        out_specs=[vmem, smem],
+        out_specs=[vmem, vmem],
         scratch_shapes=[
             pltpu.VMEM(queries.shape, queries.dtype),
             pltpu.SMEM(lengths.shape, jnp.int32),
             pltpu.VMEM(page_table.shape, jnp.int32),
-            pltpu.VMEM((1, pages), jnp.int32),
-            pltpu.SemaphoreType.DMA((4,)),
+            pltpu.SemaphoreType.DMA((3,)),
         ],
         compiler_params=pltpu.CompilerParams(vmem_limit_bytes=4 * MIB),
         cost_estimate=pl.CostEstimate(flops=2 * 10**10, bytes_accessed=64 * MIB, transcendentals=0),
@@ -160,7 +157,7 @@
     partial = pl.pallas_call(
         attend_kernel,
         out_shape=jax.ShapeDtypeStruct((requests, group + STAT_ROWS, head_dim), jnp.bfloat16),
-        in_specs=[smem, vmem, vmem, vmem],
+        in_specs=[vmem, vmem, vmem, vmem],
         out_specs=vmem,
         scratch_shapes=[
             pltpu.VMEM((pages, group, page_len), jnp.float32),
@@ -169,7 +166,7 @@
             pltpu.VMEM((requests, group, head_dim), jnp.float32),
         ],
         compiler_params=pltpu.CompilerParams(vmem_limit_bytes=24 * MIB),
-    )(pltpu.with_memory_space_constraint(code, pltpu.SMEM), query_all, key_pages, value_pages)
+    )(code, query_all, key_pages, value_pages)
     received = lax.all_to_all(partial, "pool", 0, 0, tiled=True)
     return pl.pallas_call(
         join_kernel,

time: 33.4 us -> 33.1 us (level)
    pallas_call x1, Pallas kernels: 1.65 us -> 1.13 us  [per_device(): pl.pallas_call(spread_kernel, out_shape=[jax.ShapeDtypeStruct((requests,...]
where the time goes in v6:
time: 33.1 us; the launch traced here: 33 us
  blocking collectives  28.2 us (85%)
  Pallas kernels  4.72 us (14%)
    all_to_all x1, blocking collectives, per_device(): query_all = lax.all_to_all(spread, 'pool', 0, 0, tiled=True)  16.3 us
    all_to_all x1, blocking collectives, per_device(): received = lax.all_to_all(partial, 'pool', 0, 0, tiled=True)  11.9 us
    pallas_call x1, Pallas kernels, per_device(): pl.pallas_call(attend_kernel, out_shape=jax.ShapeDtypeStruct((requests, g...  2.57 us
    pallas_call x1, Pallas kernels, per_device(): pl.pallas_call(spread_kernel, out_shape=[jax.ShapeDtypeStruct((requests,...  1.13 us
    pallas_call x1, Pallas kernels, per_device(): pl.pallas_call(join_kernel, out_shape=jax.ShapeDtypeStruct((1, 1, group *...  1.02 us

profile of v6, /device:TPU:1, one launch (start us, length us, event | category | flops | bytes accessed | tf_op | source)
XLA Modules:
  0.0 33.0 jit_solution(15728217909461847503)
XLA Ops:
  0.0 0.0 copy-start.1
  0.0 0.0 copy-start
  0.0 1.1 %shard_map.55 = (bf16[32,16,128]{2,1,0:T(8,128)(2,1)S(1)}, s32[1,64]{1,0:T(1,128)S(1)}) custom-call(bf16[1,1,2048]{2,1,0:T(2,128)(2,1)} %q_hbm.1, s32[32]{0:T(128)} %length_hbm.1, s32[32,64]{1,0:T(8,128)} %table_hbm.1), custom_call_target="tpu_custom_call" | custom-call | flops 20000000000 | bytes 67108864 | tf_op jit(solution)/shard_map/pallas_call | solution.py:139
  1.1 16.3 %all_to_all.10.q_ref = bf16[32,16,128]{2,1,0:T(8,128)(2,1)S(1)} all-to-all(bf16[32,16,128]{2,1,0:T(8,128)(2,1)S(1)} %get-tuple-element.8), channel_id=1, replica_groups=mesh['pool'=32,'head'=8] {'pool'}, dimensions={0} | all-to-all | bytes 262144 | tf_op jit(solution)/shard_map/all_to_all | solution.py:156
  17.4 0.0 copy-done.1
  17.4 0.0 copy-done
  17.4 2.6 %shard_map.56 = bf16[32,24,128]{2,1,0:T(8,128)(2,1)S(1)} custom-call(s32[1,64]{1,0:T(1,128)S(1)} %get-tuple-element.7.code_ref, bf16[32,16,128]{2,1,0:T(8,128)(2,1)S(1)} %all_to_all.10.q_ref, bf16[64,256,128]{2,1,0:T(8,128)(2,1)S(1)} %bitcast.2, bf16[64,256,128]{2,1,0:T(8,128)(2,1)S(1)} %bitcast.3), custom_call_target="tpu_custom_call" | custom-call | tf_op jit(solution)/shard_map/pallas_call | solution.py:157
  20.0 11.9 %all_to_all.11.parts_ref = bf16[32,24,128]{2,1,0:T(8,128)(2,1)S(1)} all-to-all(bf16[32,24,128]{2,1,0:T(8,128)(2,1)S(1)} %shard_map.56), channel_id=1, replica_groups=mesh['pool'=32,'head'=8] {'pool'}, dimensions={0} | all-to-all | bytes 393216 | tf_op jit(solution)/shard_map/all_to_all | solution.py:170
  31.9 1.0 %shard_map.57 = bf16[1,1,2048]{2,1,0:T(2,128)(2,1)} custom-call(bf16[32,24,128]{2,1,0:T(8,128)(2,1)S(1)} %all_to_all.11.parts_ref), custom_call_target="tpu_custom_call" | custom-call | tf_op jit(solution)/shard_map/pallas_call | solution.py:171
Async XLA Ops:
  0.0 17.4 %copy-start.1 = (bf16[64,1,256,128]{3,2,1,0:T(8,128)(2,1)S(1)}, bf16[64,1,256,128]{3,2,1,0:T(8,128)(2,1)}, u32[]{:S(2)}) copy-start(bf16[64,1,256,128]{3,2,1,0:T(8,128)(2,1)} %param.7) | copy-start | bytes 12582916
  0.0 17.4 %copy-start = (bf16[64,1,256,128]{3,2,1,0:T(8,128)(2,1)S(1)}, bf16[64,1,256,128]{3,2,1,0:T(8,128)(2,1)}, u32[]{:S(2)}) copy-start(bf16[64,1,256,128]{3,2,1,0:T(8,128)(2,1)} %param.6) | copy-start | bytes 12582916

commit v7 on v6

--- a/solution.py
+++ b/solution.py
@@ -8,7 +8,8 @@
 MASKED = -3.0e38
 EMPTY = -1.5e38
 STAT_ROWS = 8
-CODE = 512
+CODE_BITS = 9
+CODE = 1 << CODE_BITS
 PAGE = 256
 MIB = 1024 * 1024
 LOG2E = 1.4426950408889634
@@ -61,11 +62,11 @@
 
     def score(p, key_page):
         code = codes[p]
-        owner = code // CODE
+        owner = code >> CODE_BITS
         s = lax.dot_general(
             q_ref[owner], key_page, (((1,), (1,)), ((), ())), preferred_element_type=jnp.float32
         )
-        s = jnp.where(token < code % CODE, s, MASKED)
+        s = jnp.where(token < code & (CODE - 1), s, MASKED)
         s_ref[p] = s
         top = s[:, :head_dim]
         for h in range(1, halves):
@@ -77,7 +78,7 @@
     mx_ref[...] = jnp.broadcast_to(jnp.max(mx_ref[...], axis=-1, keepdims=True), mx_ref.shape)
 
     for p in range(pages):
-        owner = codes[p] // CODE
+        owner = codes[p] >> CODE_BITS
         top = mx_ref[owner]
         parts = [
             jnp.exp2((s_ref[p, :, h * head_dim : (h + 1) * head_dim] - top) * factor)

time: 33.1 us -> 33.1 us (level)
  no operation moved by 1% of the time
where the time goes in v7:
time: 33.1 us; the launch traced here: 32.9 us
  blocking collectives  28.2 us (85%)
  Pallas kernels  4.7 us (14%)
    all_to_all x1, blocking collectives, per_device(): query_all = lax.all_to_all(spread, 'pool', 0, 0, tiled=True)  16.3 us
    all_to_all x1, blocking collectives, per_device(): received = lax.all_to_all(partial, 'pool', 0, 0, tiled=True)  11.9 us
    pallas_call x1, Pallas kernels, per_device(): pl.pallas_call(attend_kernel, out_shape=jax.ShapeDtypeStruct((requests, g...  2.55 us
    pallas_call x1, Pallas kernels, per_device(): pl.pallas_call(spread_kernel, out_shape=[jax.ShapeDtypeStruct((requests,...  1.13 us
    pallas_call x1, Pallas kernels, per_device(): pl.pallas_call(join_kernel, out_shape=jax.ShapeDtypeStruct((1, 1, group *...  1.02 us

profile of v7, /device:TPU:1, one launch (start us, length us, event | category | flops | bytes accessed | tf_op | source)
XLA Modules:
  0.0 32.9 jit_solution(13634522831366399661)
XLA Ops:
  0.0 0.0 copy-start.1
  0.0 0.0 copy-start
  0.0 1.1 %shard_map.55 = (bf16[32,16,128]{2,1,0:T(8,128)(2,1)S(1)}, s32[1,64]{1,0:T(1,128)S(1)}) custom-call(bf16[1,1,2048]{2,1,0:T(2,128)(2,1)} %q_hbm.1, s32[32]{0:T(128)} %length_hbm.1, s32[32,64]{1,0:T(8,128)} %table_hbm.1), custom_call_target="tpu_custom_call" | custom-call | flops 20000000000 | bytes 67108864 | tf_op jit(solution)/shard_map/pallas_call | solution.py:140
  1.1 16.3 %all_to_all.10.q_ref = bf16[32,16,128]{2,1,0:T(8,128)(2,1)S(1)} all-to-all(bf16[32,16,128]{2,1,0:T(8,128)(2,1)S(1)} %get-tuple-element.8), channel_id=1, replica_groups=mesh['pool'=32,'head'=8] {'pool'}, dimensions={0} | all-to-all | bytes 262144 | tf_op jit(solution)/shard_map/all_to_all | solution.py:157
  17.4 0.0 copy-done.1
  17.4 0.0 copy-done
  17.4 2.6 %shard_map.56 = bf16[32,24,128]{2,1,0:T(8,128)(2,1)S(1)} custom-call(s32[1,64]{1,0:T(1,128)S(1)} %get-tuple-element.7.code_ref, bf16[32,16,128]{2,1,0:T(8,128)(2,1)S(1)} %all_to_all.10.q_ref, bf16[64,256,128]{2,1,0:T(8,128)(2,1)S(1)} %bitcast.2, bf16[64,256,128]{2,1,0:T(8,128)(2,1)S(1)} %bitcast.3), custom_call_target="tpu_custom_call" | custom-call | tf_op jit(solution)/shard_map/pallas_call | solution.py:158
  20.0 11.9 %all_to_all.11.parts_ref = bf16[32,24,128]{2,1,0:T(8,128)(2,1)S(1)} all-to-all(bf16[32,24,128]{2,1,0:T(8,128)(2,1)S(1)} %shard_map.56), channel_id=1, replica_groups=mesh['pool'=32,'head'=8] {'pool'}, dimensions={0} | all-to-all | bytes 393216 | tf_op jit(solution)/shard_map/all_to_all | solution.py:171
  31.9 1.0 %shard_map.57 = bf16[1,1,2048]{2,1,0:T(2,128)(2,1)} custom-call(bf16[32,24,128]{2,1,0:T(8,128)(2,1)S(1)} %all_to_all.11.parts_ref), custom_call_target="tpu_custom_call" | custom-call | tf_op jit(solution)/shard_map/pallas_call | solution.py:172
Async XLA Ops:
  0.0 17.4 %copy-start.1 = (bf16[64,1,256,128]{3,2,1,0:T(8,128)(2,1)S(1)}, bf16[64,1,256,128]{3,2,1,0:T(8,128)(2,1)}, u32[]{:S(2)}) copy-start(bf16[64,1,256,128]{3,2,1,0:T(8,128)(2,1)} %param.7) | copy-start | bytes 12582916
  0.0 17.4 %copy-start = (bf16[64,1,256,128]{3,2,1,0:T(8,128)(2,1)S(1)}, bf16[64,1,256,128]{3,2,1,0:T(8,128)(2,1)}, u32[]{:S(2)}) copy-start(bf16[64,1,256,128]{3,2,1,0:T(8,128)(2,1)} %param.6) | copy-start | bytes 12582916
